TPU v7x, 256 devices: a whole 4x4x8 slice. The times are simulated.
256 devices in a mesh: expert: 64 (over y, z_hi, x), zero: 4 (over z_lo, core).
Axes of the slice: x: 4, y: 4, z: 8 (z_hi: 4, z_lo: 2; z = z_hi * 2 + z_lo), core: 2. Of those that a mesh axis runs over, the one named last changes fastest.
Arguments:
- tokens: bfloat16 [32768, 3584], P(('expert', 'zero')), may hold values from -6 to 6
- accepted: int32 [32768], P(('expert', 'zero')), may hold values from 0 to 1, as said below
- routes: int32 [32768, 8], P(('expert', 'zero')), may hold values from 0 to 63, as said below
- gates: float32 [32768, 8], P(('expert', 'zero')), may hold values from 0.1 to 1
- partner: int32 [64], replicated, may hold values from 0 to 63, as said below
- w_gate: bfloat16 [64, 3584, 1024], P('expert', None, 'zero'), may hold values from -0.09375 to 0.09375
- w_up: bfloat16 [64, 3584, 1024], P('expert', None, 'zero'), may hold values from -0.09375 to 0.09375
- w_down: bfloat16 [64, 1024, 3584], P('expert', 'zero'), may hold values from -0.1875 to 0.1875
- master_rows: float32 [64, 32, 3584], P('expert', 'zero'), may hold values from -6 to 6
- first_moment: float32 [64, 32, 3584], P('expert', 'zero'), may hold values from -6 to 6
- second_moment: float32 [64, 32, 3584], P('expert', 'zero'), may hold values from 0.1 to 2
Outputs:
- combined: bfloat16 [32768, 3584], P(('expert', 'zero'))
- new_gate: bfloat16 [64, 3584, 1024], P('expert', None, 'zero')
- new_up: bfloat16 [64, 3584, 1024], P('expert', None, 'zero')
- new_down: bfloat16 [64, 1024, 3584], P('expert', 'zero')
- new_master: float32 [64, 32, 3584], P('expert', 'zero')
- new_first: float32 [64, 32, 3584], P('expert', 'zero')
- new_second: float32 [64, 32, 3584], P('expert', 'zero')
Inputs may be any that keep to these rules, and one draw needn't show every extreme that they name: `accepted`: exactly 32 rows of each device's 128 rows are 1. `routes`: each row names 8 different experts. Over the accepted rows of one device no expert is named more than 8 times, and some expert exactly 8 times. partner[partner[i]] = i, and partner[i] is i or i plus or minus 64 // 2.
All inputs are finite; a program needn't handle non-finite values.
Results may differ from a plain program's by a relative error of at most 0.0065.
Values may be sent and summed in bfloat16 or wider, within the bound.
A program may use at most 128 MiB of HBM per device.

v0:
```python
import jax
import jax.numpy as jnp
from jax import lax
from jax.sharding import PartitionSpec as P

ACC_DEV = 32


def partner_2(shard, axis, apart):
    return lax.ppermute(shard, axis, [(i, i ^ 1 << apart) for i in range(lax.axis_size(axis))])


def on_device(
    tokens,
    accepted,
    routes,
    gates,
    partner,
    w_gate,
    w_up,
    w_down,
    master_rows,
    first_moment,
    second_moment,
):
    n_expert = lax.axis_size("expert")
    my_index = lax.axis_index("expert")
    far_bit = n_expert.bit_length() - 2
    expert_ids = jnp.arange(n_expert, dtype=jnp.int32)
    mate = jnp.sum(jnp.where(expert_ids == my_index, partner, 0))
    moving = mate != my_index

    def relocate_weight(block):
        across = partner_2(block, "expert", far_bit)
        return jnp.where(moving, across, block)

    def relocate_state(block):
        across = partner_2(block.astype(jnp.bfloat16), "expert", far_bit).astype(block.dtype)
        return jnp.where(moving, across, block)

    new_gate = relocate_weight(w_gate)
    new_up = relocate_weight(w_up)
    new_down = relocate_weight(w_down)
    new_master = relocate_state(master_rows)
    new_first = relocate_state(first_moment)
    new_second = relocate_state(second_moment)
    tok_rows, topk = routes.shape
    width = tokens.shape[1]
    capacity = min(ACC_DEV, 2 * ACC_DEV * topk // n_expert)
    use_gate, use_up, use_down = (new_gate[0], new_up[0], new_down[0])
    named = routes[:, :, None] == expert_ids[None, None, :]
    target = jnp.sum(jnp.where(named, partner[None, None, :], 0), axis=-1).reshape(-1)
    keep = jnp.broadcast_to((accepted == 1)[:, None], (tok_rows, topk)).reshape(-1)
    onehot = ((target[:, None] == expert_ids[None, :]) & keep[:, None]).astype(jnp.int32)
    before = jnp.cumsum(onehot, axis=0) - onehot
    rank = jnp.sum(before * onehot, axis=-1)
    slot = target * capacity + rank
    slot_ids = jnp.arange(n_expert * capacity, dtype=jnp.int32)
    placed = (slot[None, :] == slot_ids[:, None]) & keep[None, :]
    placed = placed.reshape(n_expert * capacity, tok_rows, topk)
    place_rows = jnp.sum(placed.astype(jnp.float32), axis=-1).astype(jnp.bfloat16)
    gate_table = jnp.sum(jnp.where(placed, gates[None, :, :], jnp.float32(0.0)), axis=-1)
    outgoing = jnp.dot(place_rows, tokens, preferred_element_type=jnp.float32).astype(jnp.bfloat16)
    outgoing = outgoing.reshape(n_expert, capacity, width)
    received = lax.all_to_all(outgoing, "expert", split_axis=0, concat_axis=0, tiled=True)
    slots_here = received.shape[1]
    rows = received.reshape(-1, width)
    piece = lax.all_gather(rows, "zero", axis=0, tiled=True)
    gate_part = jnp.dot(piece, use_gate, preferred_element_type=jnp.float32)
    up_part = jnp.dot(piece, use_up, preferred_element_type=jnp.float32)
    hidden = (jax.nn.silu(gate_part) * up_part).astype(jnp.bfloat16)
    summed = lax.psum_scatter(
        jnp.dot(hidden, use_down, preferred_element_type=jnp.float32),
        "zero",
        scatter_dimension=0,
        tiled=True,
    )
    result = summed.astype(jnp.bfloat16).reshape(n_expert, slots_here, width)
    returned = lax.all_to_all(result, "expert", split_axis=0, concat_axis=0, tiled=True)
    returned = returned.reshape(n_expert * capacity, width).astype(jnp.float32)
    total = lax.dot_general(
        gate_table, returned, (((0,), (0,)), ((), ())), precision=lax.Precision.HIGHEST
    )
    combined = total.astype(jnp.bfloat16)
    return (combined, new_gate, new_up, new_down, new_master, new_first, new_second)


def solution(mesh):
    return jax.shard_map(
        on_device,
        mesh=mesh,
        in_specs=(
            P(("expert", "zero"), None),
            P(("expert", "zero")),
            P(("expert", "zero"), None),
            P(("expert", "zero"), None),
            P(),
            P("expert", None, "zero"),
            P("expert", None, "zero"),
            P("expert", "zero", None),
            P("expert", "zero", None),
            P("expert", "zero", None),
            P("expert", "zero", None),
        ),
        out_specs=(
            P(("expert", "zero"), None),
            P("expert", None, "zero"),
            P("expert", None, "zero"),
            P("expert", "zero", None),
            P("expert", "zero", None),
            P("expert", "zero", None),
            P("expert", "zero", None),
        ),
        check_vma=False,
    )
```

profile of v0, /device:TPU:32, one launch (start us, length us, event | category | flops | bytes accessed | tf_op | source)
XLA Modules:
  0.0 667.4 jit_solution(3007290071208516243)
XLA Ops:
  7.2 0.9 select_reduce_fusion.1
  8.4 0.7 broadcast_compare_fusion
  9.4 18.0 %reduce-window.6 = s32[64,8,128]{2,1,0:T(8,128)S(1)} reduce-window(s32[64,8,128]{2,1,0:T(8,128)S(1)} %fusion.19, s32[]{:T(128)} %constant.6.clone.1), window={size=1x1x128 pad=0_0x0_0x127_0}, to_apply=%region_1.2 | reduce-window | flops 8323072 | bytes 524292 | tf_op jit(solution)/shard_map/reduce-window
  28.4 1.6 convert_reduce_fusion
  30.0 1.1 fusion
  31.1 100.6 %all_to_all.10 = bf16[64,8,3584]{2,1,0:T(8,128)(2,1)} all-to-all(bf16[64,8,3584]{2,1,0:T(8,128)(2,1)S(1)} %fusion), channel_id=1, replica_groups=mesh['expert'=64,'zero'=4] {'expert'}, dimensions={0} | all-to-all | bytes 7340032 | tf_op jit(solution)/shard_map/all_to_all | solution.py:65
  131.8 1.4 copy-done.3
  133.2 0.5 collective-permute-start.2
  133.7 3.0 collective-permute-start
  136.7 0.5 collective-permute-start.1
  137.3 0.6 fusion.21
  138.6 39.2 %collective-permute-done.2 = bf16[1,256,3584]{2,1,0:T(8,128)(2,1)} collective-permute-done((bf16[1,256,3584]{2,1,0:T(8,128)(2,1)S(1)}, bf16[1,256,3584]{2,1,0:T(8,128)(2,1)}, u32[]{:S(2)}, u32[]{:S(2)}) %collective-permute-start.2) | collective-permute-done | bytes 1835040 | tf_op jit(solution)/shard_map/ppermute | solution.py:10
  177.8 2.9 broadcast_select_fusion
  180.7 36.4 %collective-permute-done = bf16[1,3584,256]{2,1,0:T(8,128)(2,1)} collective-permute-done((bf16[1,3584,256]{2,1,0:T(8,128)(2,1)}, bf16[1,3584,256]{2,1,0:T(8,128)(2,1)}, u32[]{:S(2)}, u32[]{:S(2)}) %collective-permute-start) | collective-permute-done | bytes 1835040 | tf_op jit(solution)/shard_map/ppermute | solution.py:10
  217.1 3.0 broadcast_select_fusion.2
  220.1 34.1 %collective-permute-done.1 = bf16[1,3584,256]{2,1,0:T(8,128)(2,1)} collective-permute-done((bf16[1,3584,256]{2,1,0:T(8,128)(2,1)}, bf16[1,3584,256]{2,1,0:T(8,128)(2,1)}, u32[]{:S(2)}, u32[]{:S(2)}) %collective-permute-start.1) | collective-permute-done | bytes 1835040 | tf_op jit(solution)/shard_map/ppermute | solution.py:10
  254.2 1.7 broadcast_select_fusion.1
  255.9 5.2 all-gather.2.cloned.1.call-done
  261.2 11.0 %fusion.11 = f32[2048,256]{1,0:T(8,128)} fusion(bf16[2048,3584]{1,0:T(8,128)(2,1)} %all-gather.2.cloned.1.call-done, bf16[1,3584,256]{2,1,0:T(8,128)(2,1)} %broadcast_select_fusion.2), kind=kOutput, calls=%fused_computation.14 | convolution fusion | flops 3758096384 | bytes 18612224 | tf_op jit(solution)/shard_map/dot_general | solution.py:69
  272.1 24.3 %fusion.3 = f32[2048,3584]{1,0:T(8,128)} fusion(bf16[1,256,3584]{2,1,0:T(8,128)(2,1)} %broadcast_select_fusion, f32[2048,256]{1,0:T(8,128)} %fusion.11, bf16[2048,3584]{1,0:T(8,128)(2,1)} %all-gather.2.cloned.1.call-done, bf16[1,3584,256]{2,1,0:T(8,128)(2,1)S(1)} %broadcast_select_fusion.1), kind=kOutput, calls=%fused_computation.10 | convolution fusion | flops 7519338496 | bytes 49807360 | tf_op jit(solution)/shard_map/dot_general | solution.py:73
  296.4 251.1 %reduce-scatter.2.cloned.1.call-done = f32[512,3584]{1,0:T(8,128)} async-done(((f32[2048,3584]{1,0:T(8,128)}), f32[512,3584]{1,0:T(8,128)}) %reduce-scatter.2.cloned.1.call-update) | async-done | bytes 7340048 | tf_op jit(solution)/shard_map/reduce_scatter | solution.py:72
  547.5 5.3 convert_bitcast_fusion
  552.8 13.9 %all-to-all-start.1 = ((bf16[64,8,3584]{2,1,0:T(8,128)(2,1)}), bf16[64,8,3584]{2,1,0:T(8,128)(2,1)}, u32[]{:S(2)}, u32[]{:S(2)}) async-start(bf16[64,8,3584]{2,1,0:T(8,128)(2,1)} %convert_bitcast_fusion), calls=%async_computation.2 | async-start | bytes 7340032 | tf_op jit(solution)/shard_map/all_to_all | solution.py:79
  566.8 3.2 collective-permute-start.3
  570.5 3.2 collective-permute-start.5
  573.7 1.1 collective-permute-done.3
  574.7 0.7 convert_select_fusion.2
  575.4 11.5 %collective-permute-done.4 = bf16[1,8,3584]{2,1,0:T(8,128)(2,1)S(1)} collective-permute-done((bf16[1,8,3584]{2,1,0:T(8,128)(2,1)S(1)}, bf16[1,8,3584]{2,1,0:T(8,128)(2,1)S(1)}, u32[]{:S(2)}, u32[]{:S(2)}) %collective-permute-start.4) | collective-permute-done | bytes 57376 | tf_op jit(solution)/shard_map/ppermute | solution.py:10
  586.9 0.7 convert_select_fusion.1
  587.8 0.7 convert_select_fusion
  588.5 67.3 %all-to-all-done.1 = bf16[64,8,3584]{2,1,0:T(8,128)(2,1)} async-done(((bf16[64,8,3584]{2,1,0:T(8,128)(2,1)}), bf16[64,8,3584]{2,1,0:T(8,128)(2,1)}, u32[]{:S(2)}, u32[]{:S(2)}) %all-to-all-start.1) | async-done | bytes 3670048 | tf_op jit(solution)/shard_map/all_to_all | solution.py:79
  655.8 4.7 convolution_convert_fusion.1
  (49 shorter events, 2.4 us)
Async XLA Ops:
  7.2 22.9 %copy-start = (bf16[128,3584]{1,0:T(8,128)(2,1)S(1)}, bf16[128,3584]{1,0:T(8,128)(2,1)}, u32[]{:S(2)}) copy-start(bf16[128,3584]{1,0:T(8,128)(2,1)} %param.11) | copy-start | bytes 2752516
  7.2 21.2 %copy-start.9 = (f32[128,8]{0,1:T(8,128)S(1)}, f32[128,8]{0,1:T(8,128)}, u32[]{:S(2)}) copy-start(f32[128,8]{0,1:T(8,128)} %param.14) | copy-start | bytes 12292
  7.2 254.0 %all-gather.2.cloned.1.call-start = ((), (), s32[]{:S(2)}) async-start(), calls=%async_computation.3 | async-start | bytes 18350080 | tf_op jit(solution)/shard_map/all_gather | solution.py:68
  131.7 1.5 copy-start.3
  131.7 5.6 copy-start.10
  131.7 415.8 %reduce-scatter.2.cloned.1.call-start = ((), (), s32[]{:S(2)}) async-start(), calls=%async_computation.4 | async-start | bytes 36700160 | tf_op jit(solution)/shard_map/reduce_scatter | solution.py:72
  133.2 44.6 %collective-permute-start.2 = (bf16[1,256,3584]{2,1,0:T(8,128)(2,1)S(1)}, bf16[1,256,3584]{2,1,0:T(8,128)(2,1)}, u32[]{:S(2)}, u32[]{:S(2)}) collective-permute-start(bf16[1,256,3584]{2,1,0:T(8,128)(2,1)S(1)} %copy-done.3), channel_id=1, source_target_pairs={{0,128},{4,132},{8,136},{12,140},{16,144},{20,148},{24,152},{28,15... | collective-permute-start | bytes 5505032 | tf_op jit(solution)/shard_map/ppermute | solution.py:10
  133.7 83.3 %collective-permute-start = (bf16[1,3584,256]{2,1,0:T(8,128)(2,1)}, bf16[1,3584,256]{2,1,0:T(8,128)(2,1)}, u32[]{:S(2)}, u32[]{:S(2)}) collective-permute-start(bf16[1,3584,256]{2,1,0:T(8,128)(2,1)} %param.16), channel_id=1, source_target_pairs={{0,128},{4,132},{8,136},{12,140},{16,144},{20,148},{24,152},{28,15... | collective-permute-start | bytes 5505032 | tf_op jit(solution)/shard_map/ppermute | solution.py:10
  136.7 117.4 %collective-permute-start.1 = (bf16[1,3584,256]{2,1,0:T(8,128)(2,1)}, bf16[1,3584,256]{2,1,0:T(8,128)(2,1)}, u32[]{:S(2)}, u32[]{:S(2)}) collective-permute-start(bf16[1,3584,256]{2,1,0:T(8,128)(2,1)} %param.17), channel_id=1, source_target_pairs={{0,128},{4,132},{8,136},{12,140},{16,144},{20,148},{24,152},{28,15... | collective-permute-start | bytes 5505032 | tf_op jit(solution)/shard_map/ppermute | solution.py:10
  138.6 78.5 %copy-start.4 = (bf16[1,3584,256]{2,1,0:T(8,128)(2,1)S(1)}, bf16[1,3584,256]{2,1,0:T(8,128)(2,1)}, u32[]{:S(2)}) copy-start(bf16[1,3584,256]{2,1,0:T(8,128)(2,1)} %param.16) | copy-start | bytes 5505028
  180.7 73.5 %copy-start.5 = (bf16[1,3584,256]{2,1,0:T(8,128)(2,1)S(1)}, bf16[1,3584,256]{2,1,0:T(8,128)(2,1)}, u32[]{:S(2)}) copy-start(bf16[1,3584,256]{2,1,0:T(8,128)(2,1)} %param.17) | copy-start | bytes 5505028
  255.9 16.2 %copy-start.2 = (bf16[1,3584,256]{2,1,0:T(8,128)(2,1)}, bf16[1,3584,256]{2,1,0:T(8,128)(2,1)S(1)}, u32[]{:S(2)}) copy-start(bf16[1,3584,256]{2,1,0:T(8,128)(2,1)S(1)} %broadcast_select_fusion.1) | copy-start | bytes 5505028
  552.8 13.9 %copy-start.6 = (f32[1,8,3584]{2,1,0:T(8,128)S(1)}, f32[1,8,3584]{2,1,0:T(8,128)}, u32[]{:S(2)}) copy-start(f32[1,8,3584]{2,1,0:T(8,128)} %param.19) | copy-start | bytes 344068
  552.8 17.1 %copy-start.7 = (f32[1,8,3584]{2,1,0:T(8,128)S(1)}, f32[1,8,3584]{2,1,0:T(8,128)}, u32[]{:S(2)}) copy-start(f32[1,8,3584]{2,1,0:T(8,128)} %param.20) | copy-start | bytes 344068
  552.8 17.7 %copy-start.8 = (f32[1,8,3584]{2,1,0:T(8,128)S(1)}, f32[1,8,3584]{2,1,0:T(8,128)}, u32[]{:S(2)}) copy-start(f32[1,8,3584]{2,1,0:T(8,128)} %param.21) | copy-start | bytes 344068
  552.8 103.0 %all-to-all-start.1 = ((bf16[64,8,3584]{2,1,0:T(8,128)(2,1)}), bf16[64,8,3584]{2,1,0:T(8,128)(2,1)}, u32[]{:S(2)}, u32[]{:S(2)}) async-start(bf16[64,8,3584]{2,1,0:T(8,128)(2,1)} %convert_bitcast_fusion), calls=%async_computation.2 | async-start | bytes 7340032 | tf_op jit(solution)/shard_map/all_to_all | solution.py:79
  566.8 8.0 %collective-permute-start.3 = (bf16[1,8,3584]{2,1,0:T(8,128)(2,1)S(1)}, bf16[1,8,3584]{2,1,0:T(8,128)(2,1)S(1)}, u32[]{:S(2)}, u32[]{:S(2)}) collective-permute-start(bf16[1,8,3584]{2,1,0:T(8,128)(2,1)S(1)} %convert_element_type.52), channel_id=1, source_target_pairs={{0,128},{4,132},{8,136},{12,140},{16,144},{20,148},{24,152},{28,15... | collective-permute-start | bytes 172040 | tf_op jit(solution)/shard_map/ppermute | solution.py:10
  570.0 17.0 %collective-permute-start.4 = (bf16[1,8,3584]{2,1,0:T(8,128)(2,1)S(1)}, bf16[1,8,3584]{2,1,0:T(8,128)(2,1)S(1)}, u32[]{:S(2)}, u32[]{:S(2)}) collective-permute-start(bf16[1,8,3584]{2,1,0:T(8,128)(2,1)S(1)} %convert_element_type.54), channel_id=1, source_target_pairs={{0,128},{4,132},{8,136},{12,140},{16,144},{20,148},{24,152},{28,15... | collective-permute-start | bytes 172040 | tf_op jit(solution)/shard_map/ppermute | solution.py:10
  570.5 17.3 %collective-permute-start.5 = (bf16[1,8,3584]{2,1,0:T(8,128)(2,1)S(1)}, bf16[1,8,3584]{2,1,0:T(8,128)(2,1)S(1)}, u32[]{:S(2)}, u32[]{:S(2)}) collective-permute-start(bf16[1,8,3584]{2,1,0:T(8,128)(2,1)S(1)} %convert_element_type.56), channel_id=1, source_target_pairs={{0,128},{4,132},{8,136},{12,140},{16,144},{20,148},{24,152},{28,15... | collective-permute-start | bytes 172040 | tf_op jit(solution)/shard_map/ppermute | solution.py:10
  655.8 4.7 copy-start.1
Sparse Core Ops, SparseCore 0:
  131.8 129.2 all-gather.1
  296.6 250.9 reduce-scatter.1
where the time goes:
time: 668 us; the launch traced here: 667 us
  waiting for transfers between devices  446 us (67%)
  blocking collectives  101 us (15%)
  matrix products  41.1 us (6%)
  other arithmetic  37 us (6%)
  starting transfers between devices  25 us (4%)
  between operations  14.9 us (2%)
    reduce_scatter x1, waiting for transfers between devices, on_device(): lax.psum_scatter(jnp.dot(hidden, use_down, preferred_element_type=jnp.flo...  251 us
    ppermute x6, waiting for transfers between devices, partner_2(): lax.ppermute(shard, axis, [(i, i ^ 1 << apart) for i in range(lax.axis_si...  123 us
    all_to_all x1, blocking collectives, on_device(): lax.all_to_all(outgoing, 'expert', split_axis=0, concat_axis=0, tiled=True)  101 us
    all_to_all x1, waiting for transfers between devices, on_device(): lax.all_to_all(result, 'expert', split_axis=0, concat_axis=0, tiled=True)  67.3 us
    dot_general x1, matrix products, on_device(): jnp.dot(hidden, use_down, preferred_element_type=jnp.float32)  24.3 us
    another operation x3, other arithmetic  18.2 us
    all_to_all x1, starting transfers between devices, on_device(): lax.all_to_all(result, 'expert', split_axis=0, concat_axis=0, tiled=True)  13.9 us
  transfers between devices with their start and end apart: 9, of which 9 were waited for; matrix products, arithmetic and copies ran while one was open for 2% of the time, Pallas kernels for 0%

commit v1 on v0

v1 whole, which is shorter than its diff:
```python
import functools

import jax
import jax.numpy as jnp
from jax import lax
from jax.experimental import pallas as pl
from jax.experimental.pallas import tpu as pltpu
from jax.sharding import PartitionSpec as P

MESH = pl.DeviceIdType.MESH
BF = jnp.bfloat16
F32 = jnp.float32

D = 3584
ACC = 32
CAP = 8
TOK = 128
NX, NY, NZ = 4, 4, 8
CH = NY * ACC
HALF = CH // 2
HID = 512
TILE = 512
NT = D // TILE


def rows_of(k, n=1):
    if isinstance(k, int):
        return pl.ds(k * CH, n * CH)
    return pl.ds(pl.multiple_of(k * CH, CH), n * CH)


def kernel(
    tok, acc, rt, gt, wg, wu, wd, ms, fm, sm,
    out, ng, nu, nd, nm, nf, nsd,
    w_g, w_u, w_d, gat, pck, rcv, ret, ring, fin, meta_y, meta, pick, wt_hi, wt_lo, hid,
    ys, yr, yms, ymr, zs, zr, zms, zmr, xs, xr, bs, br, is_, ir, fs, fr, ls, ws, wr, ms_s, ms_r,
):
    e = lax.axis_index("expert")
    q = lax.axis_index("zero")
    y, zh, x = e // 16, lax.rem(e // 4, 4), lax.rem(e, 4)
    zl, c = q // 2, lax.rem(q, 2)
    z = zh * 2 + zl

    def at(dy=0, dz=0, dx=0, dc=0):
        yy = lax.rem(y + dy + NY, NY)
        zz = lax.rem(z + dz + NZ, NZ)
        xx = lax.rem(x + dx + NX, NX)
        cc = lax.rem(c + dc, 2)
        return (yy * 16 + (zz // 2) * 4 + xx, lax.rem(zz, 2) * 2 + cc)

    def remote(src, dst, ssem, rsem, dev):
        return pltpu.make_async_remote_copy(src, dst, ssem, rsem, device_id=dev, device_id_type=MESH)

    barrier = pltpu.get_barrier_semaphore()
    peers = [at(dy=i) for i in (1, 2, 3)] + [at(dx=i) for i in (1, 2, 3)]
    peers += [at(dz=1), at(dz=-1), at(dc=1)]
    for dev in peers:
        pl.semaphore_signal(barrier, inc=1, device_id=dev, device_id_type=MESH)

    r128 = lax.broadcasted_iota(jnp.int32, (TOK, TOK), 0)
    c128 = lax.broadcasted_iota(jnp.int32, (TOK, TOK), 1)
    acc_row = acc[...].astype(F32)
    spread = jnp.broadcast_to(acc_row, (TOK, TOK))
    acc_col = jnp.sum(jnp.where(r128 == c128, spread, 0.0), axis=1, keepdims=True)
    rank_col = jnp.sum(jnp.where(c128 < r128, spread, 0.0), axis=1, keepdims=True)
    rank_row = jnp.sum(
        jnp.where(r128 < c128, jnp.broadcast_to(acc_col, (TOK, TOK)), 0.0), axis=0, keepdims=True
    )
    i32r = lax.broadcasted_iota(jnp.int32, (ACC, TOK), 0).astype(F32)
    sel = jnp.where((rank_row == i32r) & (acc_row > 0.5), 1.0, 0.0).astype(BF)
    pick[...] = sel
    my_rows = pl.ds(pl.multiple_of(y * ACC, ACC), ACC)
    for n in range(NT):
        cols = slice(n * TILE, (n + 1) * TILE)
        gat[my_rows, cols] = jnp.dot(sel, tok[:, cols], preferred_element_type=F32).astype(BF)
    lane = c128.astype(F32)
    sel2 = jnp.where((rank_col + (ACC * y).astype(F32) == lane) & (acc_col > 0.5), 1.0, 0.0).astype(BF)
    g_all = gt[...]
    g_hi = g_all.astype(BF).astype(F32)
    g_mid = (g_all - g_hi).astype(BF).astype(F32)
    g_lo = g_all - g_hi - g_mid
    stack = jnp.concatenate([rt[...].astype(F32), g_hi, g_mid, g_lo], axis=0).astype(BF)
    placed = jnp.dot(stack, sel2, preferred_element_type=F32)
    meta_y[0, 0:8, :] = placed[0:8]
    meta_y[0, 8:16, :] = placed[8:16] + placed[16:24] + placed[24:32]

    ring[rows_of(7), :] = jnp.zeros((CH, D), BF)
    ring[pl.ds(5 * CH + HALF, HALF), :] = jnp.zeros((HALF, D), BF)
    ring[pl.ds(6 * CH, HALF), :] = jnp.zeros((HALF, D), BF)

    pl.semaphore_wait(barrier, len(peers))

    y_copies = []
    for i in (1, 2, 3):
        dev = at(dy=i)
        y_copies.append(remote(gat.at[my_rows], gat.at[my_rows], ys.at[i - 1], yr.at[i - 1], dev))
        y_copies.append(remote(meta_y.at[0], meta_y.at[i], yms.at[i - 1], ymr.at[i - 1], dev))
    for cp in y_copies:
        cp.start()

    cols_c = pl.ds(pl.multiple_of(c * 256, 256), 256)
    w_pairs = [
        (wg.at[0], w_g.at[:, cols_c]),
        (wu.at[0], w_u.at[:, cols_c]),
        (wd.at[0], w_d.at[cols_c]),
    ]
    w_copies = []
    for i, (src, dst) in enumerate(w_pairs):
        w_copies.append(pltpu.make_async_copy(src, dst, ls.at[i]))
        w_copies.append(remote(src, dst, ws.at[i], wr.at[i], at(dc=1)))
    for cp in w_copies:
        cp.start()

    for i in (1, 2, 3):
        from_rows = pl.ds(pl.multiple_of(lax.rem(y - i + NY, NY) * ACC, ACC), ACC)
        remote(gat.at[from_rows], gat.at[from_rows], ys.at[i - 1], yr.at[i - 1], at(dy=-i)).wait_recv()
        remote(meta_y.at[0], meta_y.at[i], yms.at[i - 1], ymr.at[i - 1], at(dy=-i)).wait_recv()
    meta[0] = meta_y[0] + meta_y[1] + meta_y[2] + meta_y[3]

    def z_rows(src_k, dst_k, dz):
        return remote(gat.at[rows_of(src_k)], gat.at[rows_of(dst_k)], zs.at[dst_k], zr.at[dst_k], at(dz=dz))

    def z_meta(src_k, dst_k, dz):
        return remote(meta.at[src_k], meta.at[dst_k], zms.at[dst_k], zmr.at[dst_k], at(dz=dz))

    def z_half(which, dz):
        src = pl.ds((5 + which) * CH + which * HALF, HALF)
        dst = pl.ds(7 * CH + which * HALF, HALF)
        return remote(gat.at[src], gat.at[dst], zs.at[7 + which], zr.at[7 + which], at(dz=dz))

    for k, dz in ((1, 1), (2, -1)):
        z_rows(0, k, dz).start()
        z_meta(0, k, dz).start()

    m_copies = []
    for i, (src, dst) in enumerate(((wg, ng), (wu, nu), (wd, nd), (ms, nm), (fm, nf), (sm, nsd))):
        m_copies.append(remote(src, dst, ms_s.at[i], ms_r.at[i], at(dy=2)))
    for cp in m_copies:
        cp.start()

    base = (e - x).astype(F32)

    def x_send(k, i):
        r = pl.ds(k * CH + i * ACC, ACC) if isinstance(k, int) else pl.ds(pl.multiple_of(k * CH + i * ACC, ACC), ACC)
        return remote(pck.at[r], rcv.at[r], xs.at[k, i - 1], xr.at[k, i - 1], at(dx=i))

    def x_back(k, i):
        r = pl.ds(k * CH + i * ACC, ACC) if isinstance(k, int) else pl.ds(pl.multiple_of(k * CH + i * ACC, ACC), ACC)
        return remote(rcv.at[r], ret.at[r], bs.at[k, i - 1], br.at[k, i - 1], at(dx=-i))

    def pack(k):
        m = meta[k]
        routes, gates = m[0:8], m[8:16]
        i16 = lax.broadcasted_iota(jnp.int32, (16, CH), 0)
        want = base + lax.rem(x + i16, NX).astype(F32)
        hit = jnp.zeros((16, CH), F32)
        weight = jnp.zeros((16, CH), F32)
        for j in range(8):
            same = routes[j : j + 1] == want
            hit = hit + jnp.where(same, 1.0, 0.0)
            weight = weight + jnp.where(same, gates[j : j + 1], 0.0)
        group_r, group_c = r128 // ACC, c128 // ACC
        earlier = jnp.where((group_r == group_c) & (r128 < c128), 1.0, 0.0).astype(BF)
        rank = jnp.dot(hit.astype(BF), earlier, preferred_element_type=F32)
        lane_group = (lax.broadcasted_iota(jnp.int32, (16, CH), 1) // ACC).astype(F32)
        code = jnp.where(hit > 0.5, lane_group * CAP + rank, -1.0)
        ones, his, los = [], [], []
        for i in range(4):
            one = jnp.where(code[i : i + 1] == i32r, 1.0, 0.0)
            scaled = one * weight[i : i + 1]
            hi = scaled.astype(BF).astype(F32)
            ones.append(one)
            his.append(hi)
            los.append(scaled - hi)
        place = jnp.concatenate(ones, axis=0).astype(BF)
        wt_hi[k] = jnp.concatenate(his, axis=0).astype(BF)
        wt_lo[k] = jnp.concatenate(los, axis=0).astype(BF)
        first = k * CH if isinstance(k, int) else pl.multiple_of(k * CH, CH)

        @pl.loop(0, NT)
        def _(n):
            cols = pl.ds(pl.multiple_of(n * TILE, TILE), TILE)
            v = jnp.dot(place, gat[rows_of(k), cols], preferred_element_type=F32).astype(BF)
            rcv[pl.ds(first, ACC), cols] = v[:ACC]
            pck[pl.ds(first + ACC, CH - ACC), cols] = v[ACC:]

        for i in (1, 2, 3):
            x_send(k, i).start()

    def expert(k, n):
        for d in range(n):
            for i in (1, 2, 3):
                x_send(k + d, i).wait_recv()
        rows = rcv[rows_of(k, n), :]
        gate = jnp.dot(rows, w_g[...], preferred_element_type=F32)
        up = jnp.dot(rows, w_u[...], preferred_element_type=F32)
        hid[0 : n * CH, :] = (gate / (1.0 + jnp.exp(-gate)) * up).astype(BF)

        @pl.loop(0, NT)
        def _(t):
            cols = pl.ds(pl.multiple_of(t * TILE, TILE), TILE)
            v = jnp.dot(hid[0 : n * CH, :], w_d[:, cols], preferred_element_type=F32).astype(BF)
            rcv[rows_of(k, n), cols] = v
            for d in range(n):
                first = (k + d) * CH
                first = first if isinstance(first, int) else pl.multiple_of(first, CH)
                ret[pl.ds(first, ACC), cols] = v[d * CH : d * CH + ACC]

    def send_back(k):
        for i in (1, 2, 3):
            x_back(k, i).start()

    pack(0)
    for cp in w_copies[0::2]:
        cp.wait()
    for cp in w_copies[1::2]:
        cp.wait_recv()
    expert(0, 1)
    send_back(0)

    def step(s, carry):
        for k, dz in ((2 * s - 1, 1), (2 * s, -1)):
            z_rows(k, k, dz).wait_recv()
            z_meta(k, k, dz).wait_recv()

            @pl.when(s < 3)
            def _():
                z_rows(k, k + 2, dz).start()
                z_meta(k, k + 2, dz).start()

        @pl.when(s == 3)
        def _():
            z_half(0, 1).start()
            z_half(1, -1).start()
            z_meta(5, 7, 1).start()

        pack(2 * s - 1)
        pack(2 * s)

        @pl.when(s > 1)
        def _():
            expert(2 * s - 3, 2)

        return carry

    lax.fori_loop(1, 4, step, 0)
    z_half(0, 1).wait_recv()
    z_half(1, -1).wait_recv()
    z_meta(5, 7, 1).wait_recv()
    pack(7)
    expert(5, 2)
    expert(7, 1)
    send_back(7)
    send_back(6)

    def combine(k, slots):
        for i in (1, 2, 3):
            x_back(k, i).wait_recv()
        hi, lo = wt_hi[k], wt_lo[k]

        @pl.loop(0, NT)
        def _(n):
            cols = pl.ds(pl.multiple_of(n * TILE, TILE), TILE)
            part = ret[rows_of(k), cols]
            dims = (((0,), (0,)), ((), ()))
            v = lax.dot_general(hi, part, dims, preferred_element_type=F32)
            v = v + lax.dot_general(lo, part, dims, preferred_element_type=F32)
            for s in slots:
                v = v + ring[rows_of(s), cols].astype(F32)
            ring[rows_of(k), cols] = v.astype(BF)

    def r_rows(src_k, slot, dz):
        return remote(ring.at[rows_of(src_k)], ring.at[rows_of(slot)], is_.at[slot], ir.at[slot], at(dz=dz))

    def r_half(which, dz):
        src = pl.ds(7 * CH + which * HALF, HALF)
        dst = pl.ds((5 + which) * CH + which * HALF, HALF)
        return remote(ring.at[src], ring.at[dst], is_.at[5 + which], ir.at[5 + which], at(dz=dz))

    combine(7, (7,))
    r_half(0, -1).start()
    r_half(1, 1).start()

    def back(i, carry):
        s = 3 - i
        for k, dz in ((2 * s, 1), (2 * s - 1, -1)):

            @pl.when(k >= 2)
            def _():
                send_back(k - 1)

            @pl.when(s == 3)
            def _():
                r_half(1 if dz == 1 else 0, dz).wait_recv()

            @pl.when(s < 3)
            def _():
                r_rows(k, k, dz).wait_recv()

            combine(k, (k,))
            slot = jnp.where(k >= 3, k - 2, 0 if dz == -1 else 8)
            r_rows(k, slot, dz).start()
        return carry

    lax.fori_loop(0, 3, back, 0)
    r_rows(1, 0, -1).wait_recv()
    r_rows(2, 8, 1).wait_recv()
    combine(0, (0, 8))

    f_copies = []
    for i in (1, 2, 3):
        to_rows = pl.ds(pl.multiple_of(lax.rem(y + i, NY) * ACC, ACC), ACC)
        f_copies.append(remote(ring.at[to_rows], fin.at[i - 1], fs.at[i - 1], fr.at[i - 1], at(dy=i)))
    for cp in f_copies:
        cp.start()

    for cp in m_copies:
        cp.wait()
    for cp in w_copies[1::2]:
        cp.wait_send()
    for cp in y_copies:
        cp.wait_send()
    for k in range(1, 7):
        z_rows(0, k, 1).wait_send()
        z_meta(0, k, 1).wait_send()
    z_half(0, 1).wait_send()
    z_half(1, -1).wait_send()
    z_meta(5, 7, 1).wait_send()
    for k in range(8):
        for i in (1, 2, 3):
            x_send(k, i).wait_send()
            x_back(k, i).wait_send()
    r_half(0, -1).wait_send()
    r_half(1, 1).wait_send()
    for slot in (0, 1, 2, 3, 4, 8):
        r_rows(1, slot, 1).wait_send()

    for cp in f_copies:
        cp.wait()
    dims = (((0,), (0,)), ((), ()))
    for n in range(NT):
        cols = slice(n * TILE, (n + 1) * TILE)
        v = ring[my_rows, cols].astype(F32)
        for i in range(3):
            v = v + fin[i, :, cols].astype(F32)
        out[:, cols] = lax.dot_general(pick[...], v.astype(BF), dims, preferred_element_type=F32).astype(BF)


def on_device(tokens, accepted, routes, gates, partner, w_gate, w_up, w_down, master_rows, first_moment, second_moment):
    my_index = lax.axis_index("expert")
    ids = jnp.arange(partner.shape[0], dtype=jnp.int32)
    moving = jnp.sum(jnp.where(ids == my_index, partner, 0)) != my_index
    held = (w_gate, w_up, w_down, master_rows, first_moment, second_moment)
    vmem = pl.BlockSpec(memory_space=pltpu.VMEM)
    anywhere = pl.BlockSpec(memory_space=pl.ANY)
    dma = pltpu.SemaphoreType.DMA
    combined, *arrived = pl.pallas_call(
        kernel,
        out_shape=[jax.ShapeDtypeStruct(tokens.shape, BF)]
        + [jax.ShapeDtypeStruct(a.shape, a.dtype) for a in held],
        in_specs=[vmem] * 4 + [anywhere] * 6,
        out_specs=[vmem] + [anywhere] * 6,
        scratch_shapes=[
            pltpu.VMEM((D, HID), BF),
            pltpu.VMEM((D, HID), BF),
            pltpu.VMEM((HID, D), BF),
            pltpu.VMEM((8 * CH, D), BF),
            pltpu.VMEM((8 * CH, D), BF),
            pltpu.VMEM((8 * CH, D), BF),
            pltpu.VMEM((8 * CH, D), BF),
            pltpu.VMEM((9 * CH, D), BF),
            pltpu.VMEM((3, ACC, D), BF),
            pltpu.VMEM((4, 16, TOK), F32),
            pltpu.VMEM((8, 16, TOK), F32),
            pltpu.VMEM((ACC, TOK), BF),
            pltpu.VMEM((8, CH, CH), BF),
            pltpu.VMEM((8, CH, CH), BF),
            pltpu.VMEM((2 * CH, HID), BF),
            dma((3,)), dma((3,)), dma((3,)), dma((3,)),
            dma((9,)), dma((9,)), dma((8,)), dma((8,)),
            dma((8, 3)), dma((8, 3)), dma((8, 3)), dma((8, 3)),
            dma((9,)), dma((9,)),
            dma((3,)), dma((3,)),
            dma((3,)), dma((3,)), dma((3,)),
            dma((6,)), dma((6,)),
        ],
        compiler_params=pltpu.CompilerParams(
            collective_id=0, has_side_effects=True, vmem_limit_bytes=60 << 20
        ),
        cost_estimate=pl.CostEstimate(flops=12 * 1024 * D * HID, bytes_accessed=24 << 20, transcendentals=1024 * HID),
        name="experts",
    )(tokens, accepted.reshape(1, -1), routes.T, gates.T, *held)
    moved = tuple(jnp.where(moving, new, old) for new, old in zip(arrived, held))
    return (combined,) + moved


def solution(mesh):
    both = P(("expert", "zero"), None)
    cols = P("expert", None, "zero")
    rows = P("expert", "zero", None)
    return jax.shard_map(
        on_device,
        mesh=mesh,
        in_specs=(both, P(("expert", "zero")), both, both, P(), cols, cols, rows, rows, rows, rows),
        out_specs=(both, cols, cols, rows, rows, rows, rows),
        check_vma=False,
    )
```

time: 668 us -> 248 us (0.37)
  waiting for transfers between devices: 446 us -> 0 us
  Pallas kernels: 0 us -> 233 us
  blocking collectives: 101 us -> 0 us
  matrix products: 41.1 us -> 0 us
  other arithmetic: 37 us -> 11.6 us
  starting transfers between devices: 25 us -> 0 us
  between operations: 14.9 us -> 1.36 us
    reduce_scatter x1 -> x0, waiting for transfers between devices: 251 us -> none  [on_device(): lax.psum_scatter(jnp.dot(hidden, use_down, preferred_element_type=jnp.flo...]
    pallas_call x0 -> x1, Pallas kernels: none -> 233 us  [on_device(): pl.pallas_call(kernel, out_shape=[jax.ShapeDtypeStruct(tokens.shape, BF)]...]
    ppermute x6 -> x0, waiting for transfers between devices: 123 us -> none  [partner_2(): lax.ppermute(shard, axis, [(i, i ^ 1 << apart) for i in range(lax.axis_si...]
    all_to_all x1 -> x0, blocking collectives: 101 us -> none  [on_device(): lax.all_to_all(outgoing, 'expert', split_axis=0, concat_axis=0, tiled=True)]
    all_to_all x1 -> x0, waiting for transfers between devices: 67.3 us -> none  [on_device(): lax.all_to_all(result, 'expert', split_axis=0, concat_axis=0, tiled=True)]
    dot_general x4 -> x0, matrix products: 41.1 us -> none  [the longest x1 24.3 us: on_device(): jnp.dot(hidden, use_down, preferred_element_type=jnp.float32)]
    another operation x3 -> x0, other arithmetic: 18.2 us -> none
    all_to_all x1 -> x0, starting transfers between devices: 13.9 us -> none  [on_device(): lax.all_to_all(result, 'expert', split_axis=0, concat_axis=0, tiled=True)]
  transfers between devices with their start and end apart: 9 -> 0, of which waited for: 9 -> 0; matrix products, arithmetic and copies ran while one was open for 2% -> 0% of each run, Pallas kernels for 0% -> 0%
where the time goes in v1:
time: 248 us; the launch traced here: 247 us
  Pallas kernels  233 us (94%)
  other arithmetic  11.6 us (5%)
    pallas_call x1, Pallas kernels, on_device(): pl.pallas_call(kernel, out_shape=[jax.ShapeDtypeStruct(tokens.shape, BF)]...  233 us
    select_n x4, other arithmetic, on_device(): jnp.where(moving, new, old)  10.3 us

profile of v1, /device:TPU:32, one launch (start us, length us, event | category | flops | bytes accessed | tf_op | source)
XLA Modules:
  0.0 247.2 jit_solution(7712958244761834715)
XLA Ops:
  0.6 1.3 fusion
  2.6 0.0 copy-start.7
  2.6 0.0 copy-start.5
  2.6 0.0 copy-start.6
  2.6 0.0 copy-start
  2.6 232.6 %experts.1 = (bf16[128,3584]{1,0:T(8,128)(2,1)}, bf16[1,3584,256]{2,1,0:T(8,128)(2,1)}, bf16[1,3584,256]{2,1,0:T(8,128)(2,1)}, bf16[1,256,3584]{2,1,0:T(8,128)(2...) custom-call(bf16[128,3584]{1,0:T(8,128)(2,1)} %tok.1, s32[1,128]{1,0:T(1,128)} %bitcast.5, ...), custom_call_target="tpu_custom_call" | custom-call | flops 22548578304 | bytes 25165824 | tf_op jit(solution)/shard_map/experts/pallas_call | solution.py:357
  235.2 0.0 copy-done.7
  235.3 1.6 broadcast_select_fusion.5
  236.8 0.0 copy-done.5
  236.8 0.0 copy-done.6
  236.8 1.7 broadcast_select_fusion.3
  238.5 0.0 copy-done
  238.5 0.0 copy-start.1
  238.5 0.0 copy-start.2
  238.5 0.0 copy-start.3
  238.5 3.1 %broadcast_select_fusion = bf16[1,256,3584]{2,1,0:T(8,128)(2,1)} fusion(bf16[1,256,3584]{2,1,0:T(8,128)(2,1)} %get-tuple-element.17, bf16[1,256,3584]{2,1,0:T(8,128)(2,1)S(1)} %copy-done, pred[]{:T(512)S(6)} %ne.3), kind=kLoop, calls=%fused_computation | loop fusion | flops 917504 | bytes 5505025 | tf_op jit(solution)/shard_map/jit(_where)/select_n | solution.py:393
  241.6 0.0 copy-done.1
  241.6 0.0 copy-done.2
  241.6 0.7 copy-done.3
  242.3 0.0 copy-start.4
  242.3 4.0 %broadcast_select_fusion.1 = (bf16[1,3584,256]{2,1,0:T(8,128)(2,1)}, bf16[1,3584,256]{2,1,0:T(8,128)(2,1)}) fusion(bf16[1,3584,256]{2,1,0:T(8,128)(2,1)} %get-tuple-element.16, bf16[1,3584,256]{2,1,0:T(8,128)(2,1)S(1)} %copy-done.2, pred[]{:T(512)S(6)} %ne.3, bf16[1,3584,256]{2,1,0:T(8,128)(2,1)S(1)} %copy-done.3, bf16[1,3584,256]{2,1,0:T(8,128)(2,1)S(1)} %copy-done.1), kind=kLoop, calls=%fused_computation.1 | loop fusion | flops 1835008 | bytes 11010049 | tf_op jit(solution)/shard_map/jit(_where)/select_n | solution.py:393
  246.3 0.0 copy-done.4
  246.3 0.9 copy.19
Async XLA Ops:
  2.6 232.7 %copy-start.7 = (f32[1,8,3584]{2,1,0:T(8,128)S(1)}, f32[1,8,3584]{2,1,0:T(8,128)}, u32[]{:S(2)}) copy-start(f32[1,8,3584]{2,1,0:T(8,128)} %ms.1) | copy-start | bytes 344068
  2.6 234.2 %copy-start.5 = (f32[1,8,3584]{2,1,0:T(8,128)S(1)}, f32[1,8,3584]{2,1,0:T(8,128)}, u32[]{:S(2)}) copy-start(f32[1,8,3584]{2,1,0:T(8,128)} %fm.1) | copy-start | bytes 344068
  2.6 234.2 %copy-start.6 = (f32[1,8,3584]{2,1,0:T(8,128)S(1)}, f32[1,8,3584]{2,1,0:T(8,128)}, u32[]{:S(2)}) copy-start(f32[1,8,3584]{2,1,0:T(8,128)} %sm.1) | copy-start | bytes 344068
  2.6 235.9 %copy-start = (bf16[1,256,3584]{2,1,0:T(8,128)(2,1)S(1)}, bf16[1,256,3584]{2,1,0:T(8,128)(2,1)}, u32[]{:S(2)}) copy-start(bf16[1,256,3584]{2,1,0:T(8,128)(2,1)} %wd.1) | copy-start | bytes 5505028
  238.5 3.1 %copy-start.1 = (bf16[1,3584,256]{2,1,0:T(8,128)(2,1)S(1)}, bf16[1,3584,256]{2,1,0:T(8,128)(2,1)}, u32[]{:S(2)}) copy-start(bf16[1,3584,256]{2,1,0:T(8,128)(2,1)} %wg.1) | copy-start | bytes 5505028
  238.5 3.1 %copy-start.2 = (bf16[1,3584,256]{2,1,0:T(8,128)(2,1)S(1)}, bf16[1,3584,256]{2,1,0:T(8,128)(2,1)}, u32[]{:S(2)}) copy-start(bf16[1,3584,256]{2,1,0:T(8,128)(2,1)} %wu.1) | copy-start | bytes 5505028
  238.5 3.8 %copy-start.3 = (bf16[1,3584,256]{2,1,0:T(8,128)(2,1)S(1)}, bf16[1,3584,256]{2,1,0:T(8,128)(2,1)}, u32[]{:S(2)}) copy-start(bf16[1,3584,256]{2,1,0:T(8,128)(2,1)} %get-tuple-element.15) | copy-start | bytes 5505028
  242.3 4.0 %copy-start.4 = (bf16[128,3584]{1,0:T(8,128)(2,1)S(1)}, bf16[128,3584]{1,0:T(8,128)(2,1)}, u32[]{:S(2)}) copy-start(bf16[128,3584]{1,0:T(8,128)(2,1)} %get-tuple-element.32) | copy-start | bytes 2752516

commit v2 on v1

v2 whole, which is shorter than its diff:
```python
import functools

import jax
import jax.numpy as jnp
from jax import lax
from jax.experimental import pallas as pl
from jax.experimental.pallas import tpu as pltpu
from jax.sharding import PartitionSpec as P

MESH = pl.DeviceIdType.MESH
BF = jnp.bfloat16
F32 = jnp.float32

D = 3584
ACC = 32
CAP = 8
TOK = 128
NX, NY, NZ = 4, 4, 8
UNIT = 2 * ACC
GROUP = UNIT // 4
OWN = 7
HID = 512
TILE = 512
NT = D // TILE


def unit_rows(w, p, first=0, count=UNIT):
    if isinstance(w, int) and isinstance(p, int):
        return pl.ds((w * 8 + p) * UNIT + first, count)
    return pl.ds(pl.multiple_of((w * 8 + p) * UNIT + first, 16), count)


def ring_rows(w, slot, first=0, count=UNIT):
    if isinstance(w, int) and isinstance(slot, int):
        return pl.ds((w * 9 + slot) * UNIT + first, count)
    return pl.ds(pl.multiple_of((w * 9 + slot) * UNIT + first, 16), count)


def kernel(
    tok, acc, rt, gt, wg, wu, wd, ms, fm, sm,
    out, ng, nu, nd, nm, nf, nsd,
    w_g, w_u, w_d, gat, pck, rcv, ret, ring, fin, meta_y, meta_in, meta, pick, wt_hi, wt_lo, hid,
    ys, yr, yms, ymr, zs, zr, zms, zmr, xs, xr, bs, br, is_, ir, fs, fr, ls, ws, wr, ms_s, ms_r,
):
    e = lax.axis_index("expert")
    q = lax.axis_index("zero")
    y, zh, x = e // 16, lax.rem(e // 4, 4), lax.rem(e, 4)
    zl, c = q // 2, lax.rem(q, 2)
    z = zh * 2 + zl

    def at(dy=0, dz=0, dx=0, dc=0):
        yy = lax.rem(y + dy + NY, NY)
        zz = lax.rem(z + dz + NZ, NZ)
        xx = lax.rem(x + dx + NX, NX)
        cc = lax.rem(c + dc, 2)
        return (yy * 16 + (zz // 2) * 4 + xx, lax.rem(zz, 2) * 2 + cc)

    def remote(src, dst, ssem, rsem, dev):
        return pltpu.make_async_remote_copy(src, dst, ssem, rsem, device_id=dev, device_id_type=MESH)

    barrier = pltpu.get_barrier_semaphore()
    peers = [at(dy=i) for i in (1, 2, 3)] + [at(dx=i) for i in (1, 2, 3)]
    peers += [at(dz=1), at(dz=-1), at(dc=1)]
    for dev in peers:
        pl.semaphore_signal(barrier, inc=1, device_id=dev, device_id_type=MESH)

    r128 = lax.broadcasted_iota(jnp.int32, (TOK, TOK), 0)
    c128 = lax.broadcasted_iota(jnp.int32, (TOK, TOK), 1)
    acc_row = acc[...].astype(F32)
    spread = jnp.broadcast_to(acc_row, (TOK, TOK))
    acc_col = jnp.sum(jnp.where(r128 == c128, spread, 0.0), axis=1, keepdims=True)
    rank_col = jnp.sum(jnp.where(c128 < r128, spread, 0.0), axis=1, keepdims=True)
    rank_row = jnp.sum(
        jnp.where(r128 < c128, jnp.broadcast_to(acc_col, (TOK, TOK)), 0.0), axis=0, keepdims=True
    )
    i32r = lax.broadcasted_iota(jnp.int32, (ACC, TOK), 0).astype(F32)
    sel = jnp.where((rank_row == i32r) & (acc_row > 0.5), 1.0, 0.0).astype(BF)
    pick[...] = sel
    own_block = unit_rows(0, OWN, 0, ACC)
    for n in range(NT):
        cols = slice(n * TILE, (n + 1) * TILE)
        gat[own_block, cols] = jnp.dot(sel, tok[:, cols], preferred_element_type=F32).astype(BF)
    wide = lax.broadcasted_iota(jnp.int32, (TOK, NY * TOK), 1)
    offset = (wide // TOK) * (TOK + ACC)
    here = (rank_col + offset.astype(F32) == wide.astype(F32)) & (acc_col > 0.5)
    sel2 = jnp.where(here, 1.0, 0.0).astype(BF)
    g_all = gt[...]
    g_hi = g_all.astype(BF).astype(F32)
    g_mid = (g_all - g_hi).astype(BF).astype(F32)
    g_lo = g_all - g_hi - g_mid
    stack = jnp.concatenate([rt[...].astype(F32), g_hi, g_mid, g_lo], axis=0).astype(BF)
    placed = jnp.dot(stack, sel2, preferred_element_type=F32)
    for j in range(NY):
        part = placed[:, j * TOK : (j + 1) * TOK]
        meta_y[j, 0:8, :] = part[0:8]
        meta_y[j, 8:16, :] = part[8:16] + part[16:24] + part[24:32]

    for w in range(2):
        ring[ring_rows(w, 6), :] = jnp.zeros((UNIT, D), BF)
        ring[ring_rows(w, 4, ACC, ACC), :] = jnp.zeros((ACC, D), BF)
        ring[ring_rows(w, 5, 0, ACC), :] = jnp.zeros((ACC, D), BF)

    pl.semaphore_wait(barrier, len(peers))

    y_copies = []
    for i in (3, 2, 1):
        dev, j = at(dy=i), NY - i
        dst = unit_rows(j // 2, OWN, (j % 2) * ACC, ACC)
        y_copies.append(remote(meta_y.at[j], meta_in.at[j - 1], yms.at[j - 1], ymr.at[j - 1], dev))
        y_copies.append(remote(gat.at[own_block], gat.at[dst], ys.at[j - 1], yr.at[j - 1], dev))
    for cp in y_copies:
        cp.start()

    cols_c = pl.ds(pl.multiple_of(c * 256, 256), 256)
    w_pairs = [
        (wg.at[0], w_g.at[:, cols_c]),
        (wu.at[0], w_u.at[:, cols_c]),
        (wd.at[0], w_d.at[cols_c]),
    ]
    w_copies = []
    for i, (src, dst) in enumerate(w_pairs):
        w_copies.append(pltpu.make_async_copy(src, dst, ls.at[i]))
        w_copies.append(remote(src, dst, ws.at[i], wr.at[i], at(dc=1)))
    for cp in w_copies:
        cp.start()

    def z_rows(w, p, to, dz):
        return remote(gat.at[unit_rows(w, p)], gat.at[unit_rows(w, to)], zs.at[w, to], zr.at[w, to], at(dz=dz))

    def z_half(w, h):
        src, dst = unit_rows(w, 4 + h, h * ACC, ACC), unit_rows(w, 6, h * ACC, ACC)
        return remote(gat.at[src], gat.at[dst], zs.at[w, 6 + h], zr.at[w, 6 + h], at(dz=1 - 2 * h))

    def z_meta(p, to, dz):
        return remote(meta.at[p], meta.at[to], zms.at[to], zmr.at[to], at(dz=dz))

    def z_block(b, to, dz):
        src, dst = unit_rows(0, OWN, b * ACC, ACC), unit_rows(0, to, b * ACC, ACC)
        n = to if b == 0 else 8 + to
        return remote(gat.at[src], gat.at[dst], zs.at[0, n], zr.at[0, n], at(dz=dz))

    z_block(0, 0, 1).start()
    z_block(0, 1, -1).start()
    for i in range(0, 6, 2):
        y_copies[i].wait_recv()
    meta[OWN] = meta_y[0] + meta_in[0] + meta_in[1] + meta_in[2]
    z_meta(OWN, 0, 1).start()
    z_meta(OWN, 1, -1).start()
    y_copies[1].wait_recv()
    z_block(1, 0, 1).start()
    z_block(1, 1, -1).start()

    base = (e - x).astype(F32)

    def x_send(w, p, i):
        r = unit_rows(w, p, i * GROUP, GROUP)
        return remote(pck.at[r], rcv.at[r], xs.at[w * 8 + p, i - 1], xr.at[w * 8 + p, i - 1], at(dx=i))

    def x_back(w, p, i):
        r = unit_rows(w, p, i * GROUP, GROUP)
        return remote(rcv.at[r], ret.at[r], bs.at[w * 8 + p, i - 1], br.at[w * 8 + p, i - 1], at(dx=-i))

    def pack(w, p):
        m = meta[p]
        m = jnp.where(w == 0, m, pltpu.roll(m, UNIT, 1))
        routes, gates = m[0:8], m[8:16]
        i16 = lax.broadcasted_iota(jnp.int32, (16, TOK), 0)
        want = base + lax.rem(x + i16, NX).astype(F32)
        hit = jnp.zeros((16, TOK), F32)
        weight = jnp.zeros((16, TOK), F32)
        for j in range(8):
            same = routes[j : j + 1] == want
            hit = hit + jnp.where(same, 1.0, 0.0)
            weight = weight + jnp.where(same, gates[j : j + 1], 0.0)
        earlier = jnp.where((r128 // ACC == c128 // ACC) & (r128 < c128), 1.0, 0.0).astype(BF)
        rank = jnp.dot(hit.astype(BF), earlier, preferred_element_type=F32)
        lane_group = (lax.broadcasted_iota(jnp.int32, (16, TOK), 1) // ACC).astype(F32)
        code = jnp.where(hit > 0.5, lane_group * CAP + rank, -1.0)
        ones, his, los = [], [], []
        for i in range(4):
            one = jnp.where(code[i : i + 1] == i32r[0:GROUP], 1.0, 0.0)
            scaled = one * weight[i : i + 1]
            hi = scaled.astype(BF).astype(F32)
            ones.append(one)
            his.append(hi)
            los.append(scaled - hi)
        place = jnp.concatenate(ones, axis=0).astype(BF)[:, 0:UNIT]
        wt_hi[w * 8 + p] = jnp.concatenate(his, axis=0).astype(BF)
        wt_lo[w * 8 + p] = jnp.concatenate(los, axis=0).astype(BF)

        @pl.loop(0, NT)
        def _(n):
            cols = pl.ds(pl.multiple_of(n * TILE, TILE), TILE)
            v = jnp.dot(place, gat[unit_rows(w, p), cols], preferred_element_type=F32).astype(BF)
            rcv[unit_rows(w, p, 0, GROUP), cols] = v[:GROUP]
            pck[unit_rows(w, p, GROUP, UNIT - GROUP), cols] = v[GROUP:]

        for i in (1, 2, 3):
            x_send(w, p, i).start()

    def expert(w, p):
        for d in range(2):
            for i in (1, 2, 3):
                x_send(w, p + d, i).wait_recv()
        rows = rcv[unit_rows(w, p, 0, 2 * UNIT), :]
        gate = jnp.dot(rows, w_g[...], preferred_element_type=F32)
        up = jnp.dot(rows, w_u[...], preferred_element_type=F32)
        hid[...] = (gate / (1.0 + jnp.exp(-gate)) * up).astype(BF)

        @pl.loop(0, NT)
        def _(t):
            cols = pl.ds(pl.multiple_of(t * TILE, TILE), TILE)
            v = jnp.dot(hid[...], w_d[:, cols], preferred_element_type=F32).astype(BF)
            rcv[unit_rows(w, p, 0, 2 * UNIT), cols] = v
            for d in range(2):
                ret[unit_rows(w, p + d, 0, GROUP), cols] = v[d * UNIT : d * UNIT + GROUP]

    def send_back(w, p):
        for i in (1, 2, 3):
            x_back(w, p, i).start()

    def combine(w, p, slots):
        for i in (1, 2, 3):
            x_back(w, p, i).wait_recv()
        hi, lo = wt_hi[w * 8 + p][:, 0:UNIT], wt_lo[w * 8 + p][:, 0:UNIT]

        @pl.loop(0, NT)
        def _(n):
            cols = pl.ds(pl.multiple_of(n * TILE, TILE), TILE)
            part = ret[unit_rows(w, p), cols]
            dims = (((0,), (0,)), ((), ()))
            v = lax.dot_general(hi, part, dims, preferred_element_type=F32)
            v = v + lax.dot_general(lo, part, dims, preferred_element_type=F32)
            for s in slots:
                v = v + ring[ring_rows(w, s), cols].astype(F32)
            ring[ring_rows(w, slots[0]), cols] = v.astype(BF)

    def r_rows(w, p, to, dz):
        return remote(ring.at[ring_rows(w, p)], ring.at[ring_rows(w, to)], is_.at[w, to], ir.at[w, to], at(dz=dz))

    def r_half(w, h):
        src, dst = ring_rows(w, 6, h * ACC, ACC), ring_rows(w, 4 + h, h * ACC, ACC)
        return remote(ring.at[src], ring.at[dst], is_.at[w, 4 + h], ir.at[w, 4 + h], at(dz=2 * h - 1))

    def y_sum(j):
        src = ring_rows(j // 2, OWN, (j % 2) * ACC, ACC)
        return remote(ring.at[src], fin.at[j - 1], fs.at[j - 1], fr.at[j - 1], at(dy=j))

    pack(0, OWN)

    m_copies = []
    for i, (src, dst) in enumerate(((wg, ng), (wu, nu), (wd, nd), (ms, nm), (fm, nf), (sm, nsd))):
        m_copies.append(remote(src, dst, ms_s.at[i], ms_r.at[i], at(dy=2)))
    for cp in m_copies:
        cp.start()

    y_copies[3].wait_recv()
    y_copies[5].wait_recv()
    pack(1, OWN)
    for cp in w_copies[0::2]:
        cp.wait()
    for cp in w_copies[1::2]:
        cp.wait_recv()

    def tick(i, carry):
        w = jnp.where(i > 4, 1, 0)
        s = i - 4 * w
        first = 2 * s - 2

        @pl.when((i <= 8) & (s <= 3))
        def _():
            for h in range(2):
                dz = 1 - 2 * h

                @pl.when(i == 1)
                def _():
                    z_block(0, h, dz).wait_recv()
                    z_block(1, h, dz).wait_recv()

                @pl.when(i > 1)
                def _():
                    z_rows(w, first + h, first + h, dz).wait_recv()

                @pl.when(s < 3)
                def _():
                    z_rows(w, first + h, first + h + 2, dz).start()

                @pl.when(s == 3)
                def _():
                    z_half(w, h).start()

            @pl.when(i == 3)
            def _():
                z_rows(1, OWN, 0, 1).start()
                z_rows(1, OWN, 1, -1).start()

            @pl.when(i <= 3)
            def _():
                for h in range(2):
                    dz = 1 - 2 * h
                    z_meta(first + h, first + h, dz).wait_recv()

                    @pl.when(s < 3)
                    def _():
                        z_meta(first + h, first + h + 2, dz).start()

                @pl.when(s == 3)
                def _():
                    z_meta(4, 6, 1).start()

        @pl.when((i <= 8) & (s == 4))
        def _():
            z_half(w, 0).wait_recv()
            z_half(w, 1).wait_recv()

            @pl.when(i == 4)
            def _():
                z_meta(4, 6, 1).wait_recv()

        @pl.when(i <= 8)
        def _():
            @pl.loop(0, jnp.where(s == 4, 1, 2))
            def _(d):
                pack(w, first + d)

        @pl.when(i >= 9)
        def _():
            send_back_step(i - 9)

        @pl.when(i >= 3)
        def _():
            we = jnp.where(i > 6, 1, 0)
            expert(we, 2 * (i - 2 - 4 * we) - 2)

        return carry

    def wave_and_distance(r):
        w = jnp.where(r < 4, r // 2, lax.rem(r, 2))
        return w, jnp.where(r < 4, 4 - lax.rem(r, 2), 4 - r // 2)

    def send_back_step(r):
        w, s = wave_and_distance(r)

        @pl.when((r < 8) & (s == 4))
        def _():
            send_back(w, 6)

        @pl.when((r < 8) & (s < 4))
        def _():
            send_back(w, 2 * s - 1)
            send_back(w, 2 * s - 2)

        @pl.when(r >= 8)
        def _():
            send_back(r - 8, OWN)

    def return_step(r, carry):
        w, s = wave_and_distance(r)
        send_back_step(r + 2)

        @pl.when(s == 4)
        def _():
            combine(w, 6, (6,))
            r_half(w, 0).start()
            r_half(w, 1).start()

        @pl.when(s < 4)
        def _():
            @pl.loop(0, 2)
            def _(h):
                p = 2 * s - 1 - h
                dz = 1 - 2 * h

                @pl.when(s == 3)
                def _():
                    r_half(w, 1 - h).wait_recv()

                @pl.when(s < 3)
                def _():
                    r_rows(w, p, p, dz).wait_recv()

                combine(w, p, (p,))
                r_rows(w, p, jnp.where(p >= 2, p - 2, OWN + p), dz).start()

        return carry

    lax.fori_loop(1, 11, tick, 0)
    lax.fori_loop(0, 8, return_step, 0)

    @pl.loop(0, 2)
    def _(w):
        r_rows(w, 0, OWN, -1).wait_recv()
        r_rows(w, 1, OWN + 1, 1).wait_recv()
        combine(w, OWN, (OWN, OWN + 1))

        @pl.when(w == 0)
        def _():
            y_sum(1).start()

    y_sum(2).start()
    y_sum(3).start()

    for cp in m_copies:
        cp.wait()
    for cp in w_copies[1::2]:
        cp.wait_send()
    for cp in y_copies:
        cp.wait_send()
    for p in range(7):
        z_meta(OWN, p, 1).wait_send()
    for p in range(2):
        z_rows(1, OWN, p, 1).wait_send()
        for b in range(2):
            z_block(b, p, 1).wait_send()

    @pl.loop(0, 2)
    def _(w):
        for p in range(2, 6):
            z_rows(w, OWN, p, 1).wait_send()
        for h in range(2):
            z_half(w, h).wait_send()
            r_half(w, h).wait_send()
        for slot in (0, 1, 2, 3, OWN, OWN + 1):
            r_rows(w, 0, slot, 1).wait_send()

        @pl.loop(0, 8)
        def _(p):
            for i in (1, 2, 3):
                x_send(w, p, i).wait_send()
                x_back(w, p, i).wait_send()

    for j in (1, 2, 3):
        y_sum(j).wait()
    dims = (((0,), (0,)), ((), ()))
    for n in range(NT):
        cols = slice(n * TILE, (n + 1) * TILE)
        v = ring[ring_rows(0, OWN, 0, ACC), cols].astype(F32)
        for i in range(3):
            v = v + fin[i, :, cols].astype(F32)
        out[:, cols] = lax.dot_general(pick[...], v.astype(BF), dims, preferred_element_type=F32).astype(BF)


def on_device(tokens, accepted, routes, gates, partner, w_gate, w_up, w_down, master_rows, first_moment, second_moment):
    my_index = lax.axis_index("expert")
    ids = jnp.arange(partner.shape[0], dtype=jnp.int32)
    moving = jnp.sum(jnp.where(ids == my_index, partner, 0)) != my_index
    held = (w_gate, w_up, w_down, master_rows, first_moment, second_moment)
    vmem = pl.BlockSpec(memory_space=pltpu.VMEM)
    anywhere = pl.BlockSpec(memory_space=pl.ANY)
    dma = pltpu.SemaphoreType.DMA
    combined, *arrived = pl.pallas_call(
        kernel,
        out_shape=[jax.ShapeDtypeStruct(tokens.shape, BF)]
        + [jax.ShapeDtypeStruct(a.shape, a.dtype) for a in held],
        in_specs=[vmem] * 4 + [anywhere] * 6,
        out_specs=[vmem] + [anywhere] * 6,
        scratch_shapes=[
            pltpu.VMEM((D, HID), BF),
            pltpu.VMEM((D, HID), BF),
            pltpu.VMEM((HID, D), BF),
            pltpu.VMEM((16 * UNIT, D), BF),
            pltpu.VMEM((16 * UNIT, D), BF),
            pltpu.VMEM((16 * UNIT, D), BF),
            pltpu.VMEM((16 * UNIT, D), BF),
            pltpu.VMEM((18 * UNIT, D), BF),
            pltpu.VMEM((3, ACC, D), BF),
            pltpu.VMEM((4, 16, TOK), F32),
            pltpu.VMEM((3, 16, TOK), F32),
            pltpu.VMEM((8, 16, TOK), F32),
            pltpu.VMEM((ACC, TOK), BF),
            pltpu.VMEM((16, UNIT, TOK), BF),
            pltpu.VMEM((16, UNIT, TOK), BF),
            pltpu.VMEM((2 * UNIT, HID), BF),
            dma((3,)), dma((3,)), dma((3,)), dma((3,)),
            dma((2, 10)), dma((2, 10)), dma((7,)), dma((7,)),
            dma((16, 3)), dma((16, 3)), dma((16, 3)), dma((16, 3)),
            dma((2, 9)), dma((2, 9)),
            dma((3,)), dma((3,)),
            dma((3,)), dma((3,)), dma((3,)),
            dma((6,)), dma((6,)),
        ],
        compiler_params=pltpu.CompilerParams(
            collective_id=0, has_side_effects=True, vmem_limit_bytes=60 << 20
        ),
        cost_estimate=pl.CostEstimate(flops=12 * 1024 * D * HID, bytes_accessed=24 << 20, transcendentals=1024 * HID),
        name="experts",
    )(tokens, accepted.reshape(1, -1), routes.T, gates.T, *held)
    moved = [jnp.where(moving, new, old) for new, old in zip(arrived, held)]
    return (combined, *moved)


def solution(mesh):
    both = P(("expert", "zero"), None)
    cols = P("expert", None, "zero")
    rows = P("expert", "zero", None)
    return jax.shard_map(
        on_device,
        mesh=mesh,
        in_specs=(both, P(("expert", "zero")), both, both, P(), cols, cols, rows, rows, rows, rows),
        out_specs=(both, cols, cols, rows, rows, rows, rows),
        check_vma=False,
    )
```

time: 248 us -> 212 us (0.85)
  Pallas kernels: 233 us -> 196 us
    pallas_call x1, Pallas kernels: 233 us -> 196 us  [on_device(): pl.pallas_call(kernel, out_shape=[jax.ShapeDtypeStruct(tokens.shape, BF)]...]
where the time goes in v2:
time: 212 us; the launch traced here: 211 us
  Pallas kernels  196 us (92%)
  other arithmetic  11.6 us (5%)
    pallas_call x1, Pallas kernels, on_device(): pl.pallas_call(kernel, out_shape=[jax.ShapeDtypeStruct(tokens.shape, BF)]...  196 us
    select_n x4, other arithmetic, on_device(): moved = [jnp.where(moving, new, old) for new, old in zip(arrived, held)]  10.3 us

profile of v2, /device:TPU:32, one launch (start us, length us, event | category | flops | bytes accessed | tf_op | source)
XLA Modules:
  0.0 211.0 jit_solution(2451235939912305104)
XLA Ops:
  0.6 1.3 fusion
  2.6 0.0 copy-start.7
  2.6 0.0 copy-start.5
  2.6 0.0 copy-start.6
  2.6 0.0 copy-start
  2.6 196.3 %experts.1 = (bf16[128,3584]{1,0:T(8,128)(2,1)}, bf16[1,3584,256]{2,1,0:T(8,128)(2,1)}, bf16[1,3584,256]{2,1,0:T(8,128)(2,1)}, bf16[1,256,3584]{2,1,0:T(8,128)(2...) custom-call(bf16[128,3584]{1,0:T(8,128)(2,1)} %tok.1, s32[1,128]{1,0:T(1,128)} %bitcast.5, ...), custom_call_target="tpu_custom_call" | custom-call | flops 22548578304 | bytes 25165824 | tf_op jit(solution)/shard_map/experts/pallas_call | solution.py:451
  199.0 0.0 copy-done.7
  199.0 1.6 broadcast_select_fusion.5
  200.6 0.0 copy-done.5
  200.6 0.0 copy-done.6
  200.6 1.7 broadcast_select_fusion.3
  202.2 0.0 copy-done
  202.2 0.0 copy-start.1
  202.2 0.0 copy-start.2
  202.2 0.0 copy-start.3
  202.2 3.1 %broadcast_select_fusion = bf16[1,256,3584]{2,1,0:T(8,128)(2,1)} fusion(bf16[1,256,3584]{2,1,0:T(8,128)(2,1)} %get-tuple-element.17, bf16[1,256,3584]{2,1,0:T(8,128)(2,1)S(1)} %copy-done, pred[]{:T(512)S(6)} %ne.3), kind=kLoop, calls=%fused_computation | loop fusion | flops 917504 | bytes 5505025 | tf_op jit(solution)/shard_map/jit(_where)/select_n | solution.py:488
  205.3 0.0 copy-done.1
  205.3 0.0 copy-done.2
  205.3 0.7 copy-done.3
  206.0 0.0 copy-start.4
  206.0 4.0 %broadcast_select_fusion.1 = (bf16[1,3584,256]{2,1,0:T(8,128)(2,1)}, bf16[1,3584,256]{2,1,0:T(8,128)(2,1)}) fusion(bf16[1,3584,256]{2,1,0:T(8,128)(2,1)} %get-tuple-element.16, bf16[1,3584,256]{2,1,0:T(8,128)(2,1)S(1)} %copy-done.2, pred[]{:T(512)S(6)} %ne.3, bf16[1,3584,256]{2,1,0:T(8,128)(2,1)S(1)} %copy-done.3, bf16[1,3584,256]{2,1,0:T(8,128)(2,1)S(1)} %copy-done.1), kind=kLoop, calls=%fused_computation.1 | loop fusion | flops 1835008 | bytes 11010049 | tf_op jit(solution)/shard_map/jit(_where)/select_n | solution.py:488
  210.0 0.0 copy-done.4
  210.1 0.9 copy.19
Async XLA Ops:
  2.6 196.4 %copy-start.7 = (f32[1,8,3584]{2,1,0:T(8,128)S(1)}, f32[1,8,3584]{2,1,0:T(8,128)}, u32[]{:S(2)}) copy-start(f32[1,8,3584]{2,1,0:T(8,128)} %ms.1) | copy-start | bytes 344068
  2.6 198.0 %copy-start.5 = (f32[1,8,3584]{2,1,0:T(8,128)S(1)}, f32[1,8,3584]{2,1,0:T(8,128)}, u32[]{:S(2)}) copy-start(f32[1,8,3584]{2,1,0:T(8,128)} %fm.1) | copy-start | bytes 344068
  2.6 198.0 %copy-start.6 = (f32[1,8,3584]{2,1,0:T(8,128)S(1)}, f32[1,8,3584]{2,1,0:T(8,128)}, u32[]{:S(2)}) copy-start(f32[1,8,3584]{2,1,0:T(8,128)} %sm.1) | copy-start | bytes 344068
  2.6 199.6 %copy-start = (bf16[1,256,3584]{2,1,0:T(8,128)(2,1)S(1)}, bf16[1,256,3584]{2,1,0:T(8,128)(2,1)}, u32[]{:S(2)}) copy-start(bf16[1,256,3584]{2,1,0:T(8,128)(2,1)} %wd.1) | copy-start | bytes 5505028
  202.2 3.1 %copy-start.1 = (bf16[1,3584,256]{2,1,0:T(8,128)(2,1)S(1)}, bf16[1,3584,256]{2,1,0:T(8,128)(2,1)}, u32[]{:S(2)}) copy-start(bf16[1,3584,256]{2,1,0:T(8,128)(2,1)} %wg.1) | copy-start | bytes 5505028
  202.2 3.1 %copy-start.2 = (bf16[1,3584,256]{2,1,0:T(8,128)(2,1)S(1)}, bf16[1,3584,256]{2,1,0:T(8,128)(2,1)}, u32[]{:S(2)}) copy-start(bf16[1,3584,256]{2,1,0:T(8,128)(2,1)} %wu.1) | copy-start | bytes 5505028
  202.2 3.8 %copy-start.3 = (bf16[1,3584,256]{2,1,0:T(8,128)(2,1)S(1)}, bf16[1,3584,256]{2,1,0:T(8,128)(2,1)}, u32[]{:S(2)}) copy-start(bf16[1,3584,256]{2,1,0:T(8,128)(2,1)} %get-tuple-element.15) | copy-start | bytes 5505028
  206.0 4.0 %copy-start.4 = (bf16[128,3584]{1,0:T(8,128)(2,1)S(1)}, bf16[128,3584]{1,0:T(8,128)(2,1)}, u32[]{:S(2)}) copy-start(bf16[128,3584]{1,0:T(8,128)(2,1)} %get-tuple-element.32) | copy-start | bytes 2752516

commit v3 on v2

--- a/solution.py
+++ b/solution.py
@@ -19,8 +19,9 @@
 UNIT = 2 * ACC
 GROUP = UNIT // 4
 OWN = 7
+STEP = (0, 2, 1, 3)
 HID = 512
-TILE = 512
+TILE = 1792
 NT = D // TILE
 
 
@@ -102,13 +103,14 @@
 
     pl.semaphore_wait(barrier, len(peers))
 
-    y_copies = []
-    for i in (3, 2, 1):
-        dev, j = at(dy=i), NY - i
-        dst = unit_rows(j // 2, OWN, (j % 2) * ACC, ACC)
-        y_copies.append(remote(meta_y.at[j], meta_in.at[j - 1], yms.at[j - 1], ymr.at[j - 1], dev))
-        y_copies.append(remote(gat.at[own_block], gat.at[dst], ys.at[j - 1], yr.at[j - 1], dev))
-    for cp in y_copies:
+    y_meta, y_rows = [], []
+    for n in (1, 2, 3):
+        dev = at(dy=-STEP[n])
+        dst = unit_rows(n // 2, OWN, (n % 2) * ACC, ACC)
+        y_meta.append(remote(meta_y.at[n], meta_in.at[n - 1], yms.at[n - 1], ymr.at[n - 1], dev))
+        y_rows.append(remote(gat.at[own_block], gat.at[dst], ys.at[n - 1], yr.at[n - 1], dev))
+    y_rows[0].start()
+    for cp in y_meta:
         cp.start()
 
     cols_c = pl.ds(pl.multiple_of(c * 256, 256), 256)
@@ -141,14 +143,16 @@
 
     z_block(0, 0, 1).start()
     z_block(0, 1, -1).start()
-    for i in range(0, 6, 2):
-        y_copies[i].wait_recv()
+    for cp in y_meta:
+        cp.wait_recv()
     meta[OWN] = meta_y[0] + meta_in[0] + meta_in[1] + meta_in[2]
     z_meta(OWN, 0, 1).start()
     z_meta(OWN, 1, -1).start()
-    y_copies[1].wait_recv()
+    y_rows[0].wait_recv()
     z_block(1, 0, 1).start()
     z_block(1, 1, -1).start()
+    for cp in y_rows[1:]:
+        cp.start()
 
     base = (e - x).astype(F32)
 
@@ -242,9 +246,9 @@
         src, dst = ring_rows(w, 6, h * ACC, ACC), ring_rows(w, 4 + h, h * ACC, ACC)
         return remote(ring.at[src], ring.at[dst], is_.at[w, 4 + h], ir.at[w, 4 + h], at(dz=2 * h - 1))
 
-    def y_sum(j):
-        src = ring_rows(j // 2, OWN, (j % 2) * ACC, ACC)
-        return remote(ring.at[src], fin.at[j - 1], fs.at[j - 1], fr.at[j - 1], at(dy=j))
+    def y_sum(n):
+        src = ring_rows(n // 2, OWN, (n % 2) * ACC, ACC)
+        return remote(ring.at[src], fin.at[n - 1], fs.at[n - 1], fr.at[n - 1], at(dy=STEP[n]))
 
     pack(0, OWN)
 
@@ -254,8 +258,8 @@
     for cp in m_copies:
         cp.start()
 
-    y_copies[3].wait_recv()
-    y_copies[5].wait_recv()
+    for cp in y_rows[1:]:
+        cp.wait_recv()
     pack(1, OWN)
     for cp in w_copies[0::2]:
         cp.wait()
@@ -404,7 +408,7 @@
         cp.wait()
     for cp in w_copies[1::2]:
         cp.wait_send()
-    for cp in y_copies:
+    for cp in y_meta + y_rows:
         cp.wait_send()
     for p in range(7):
         z_meta(OWN, p, 1).wait_send()
@@ -429,8 +433,8 @@
                 x_send(w, p, i).wait_send()
                 x_back(w, p, i).wait_send()
 
-    for j in (1, 2, 3):
-        y_sum(j).wait()
+    for n in (1, 2, 3):
+        y_sum(n).wait()
     dims = (((0,), (0,)), ((), ()))
     for n in range(NT):
         cols = slice(n * TILE, (n + 1) * TILE)
@@ -440,10 +444,38 @@
         out[:, cols] = lax.dot_general(pick[...], v.astype(BF), dims, preferred_element_type=F32).astype(BF)
 
 
+def pieces(shape):
+    lead, rows = (0,) * (len(shape) - 2), shape[-2]
+    parts = 4 if rows % 64 == 0 else 1
+    return [lead + (slice(i * rows // parts, (i + 1) * rows // parts),) for i in range(parts)]
+
+
+def select(count, partner, *refs):
+    arrived, held, whole = refs[:count], refs[count : 2 * count], refs[2 * count]
+    outs = refs[2 * count + 1 : 3 * count + 2]
+    stage, (loads, stores) = refs[3 * count + 2 : -2], refs[-2:]
+    me = lax.axis_index("expert")
+    moving = partner[me] != me
+    work = [(a, i) for a in range(count + 1) for i in pieces(outs[a].shape)]
+
+    def load(sources):
+        for n, (a, i) in enumerate(work):
+            if a < count:
+                pltpu.make_async_copy(sources[a].at[i], stage[a].at[i], loads.at[n]).start()
+
+    pl.when(moving)(lambda: load(arrived))
+    pl.when(jnp.logical_not(moving))(lambda: load(held))
+    for n, (a, i) in enumerate(work):
+        if a == count:
+            pltpu.make_async_copy(whole.at[i], stage[a].at[i], loads.at[n]).start()
+    for n, (a, i) in enumerate(work):
+        pltpu.make_async_copy(outs[a].at[i], stage[a].at[i], loads.at[n]).wait()
+        pltpu.make_async_copy(stage[a].at[i], outs[a].at[i], stores.at[n]).start()
+    for n, (a, i) in enumerate(work):
+        pltpu.make_async_copy(stage[a].at[i], outs[a].at[i], stores.at[n]).wait()
+
+
 def on_device(tokens, accepted, routes, gates, partner, w_gate, w_up, w_down, master_rows, first_moment, second_moment):
-    my_index = lax.axis_index("expert")
-    ids = jnp.arange(partner.shape[0], dtype=jnp.int32)
-    moving = jnp.sum(jnp.where(ids == my_index, partner, 0)) != my_index
     held = (w_gate, w_up, w_down, master_rows, first_moment, second_moment)
     vmem = pl.BlockSpec(memory_space=pltpu.VMEM)
     anywhere = pl.BlockSpec(memory_space=pl.ANY)
@@ -485,7 +517,19 @@
         cost_estimate=pl.CostEstimate(flops=12 * 1024 * D * HID, bytes_accessed=24 << 20, transcendentals=1024 * HID),
         name="experts",
     )(tokens, accepted.reshape(1, -1), routes.T, gates.T, *held)
-    moved = [jnp.where(moving, new, old) for new, old in zip(arrived, held)]
+    count = len(held)
+    hbm = pl.BlockSpec(memory_space=pltpu.HBM)
+    outs = [jax.ShapeDtypeStruct(a.shape, a.dtype) for a in (*held, combined)]
+    work = sum(len(pieces(a.shape)) for a in outs)
+    *moved, combined = pl.pallas_call(
+        functools.partial(select, count),
+        out_shape=outs,
+        in_specs=[pl.BlockSpec(memory_space=pltpu.SMEM)] + [hbm] * (2 * count + 1),
+        out_specs=[hbm] * (count + 1),
+        scratch_shapes=[pltpu.VMEM(a.shape, a.dtype) for a in outs] + [dma((work,)), dma((work,))],
+        compiler_params=pltpu.CompilerParams(vmem_limit_bytes=60 << 20),
+        name="select",
+    )(partner, *arrived, *held, combined)
     return (combined, *moved)
 
 

time: 212 us -> 199 us (0.939)
  other arithmetic: 11.6 us -> 0 us
    select_n x4 -> x0, other arithmetic: 10.3 us -> none  [on_device(): moved = [jnp.where(moving, new, old) for new, old in zip(arrived, held)]]
    pallas_call x0 -> x1, Pallas kernels: none -> 6.38 us  [on_device(): pl.pallas_call(functools.partial(select, count), out_shape=outs, in_specs...]
    pallas_call x1, Pallas kernels: 196 us -> 191 us  [on_device(): pl.pallas_call(kernel, out_shape=[jax.ShapeDtypeStruct(tokens.shape, BF)]...]
where the time goes in v3:
time: 199 us; the launch traced here: 198 us
  Pallas kernels  198 us (99%)
    pallas_call x1, Pallas kernels, on_device(): pl.pallas_call(kernel, out_shape=[jax.ShapeDtypeStruct(tokens.shape, BF)]...  191 us
    pallas_call x1, Pallas kernels, on_device(): pl.pallas_call(functools.partial(select, count), out_shape=outs, in_specs...  6.38 us

profile of v3, /device:TPU:32, one launch (start us, length us, event | category | flops | bytes accessed | tf_op | source)
XLA Modules:
  0.0 198.2 jit_solution(3249421534721994803)
XLA Ops:
  0.6 191.2 %experts.1 = (bf16[128,3584]{1,0:T(8,128)(2,1)}, bf16[1,3584,256]{2,1,0:T(8,128)(2,1)}, bf16[1,3584,256]{2,1,0:T(8,128)(2,1)}, bf16[1,256,3584]{2,1,0:T(8,128)(2...) custom-call(bf16[128,3584]{1,0:T(8,128)(2,1)} %tok.1, s32[1,128]{1,0:T(1,128)} %bitcast.5, ...), custom_call_target="tpu_custom_call" | custom-call | flops 22548578304 | bytes 25165824 | tf_op jit(solution)/shard_map/experts/pallas_call | solution.py:483
  191.8 6.4 %select.1 = (bf16[1,3584,256]{2,1,0:T(8,128)(2,1)}, bf16[1,3584,256]{2,1,0:T(8,128)(2,1)}, bf16[1,256,3584]{2,1,0:T(8,128)(2,1)}, f32[1,8,3584]{2,1,0:T(8,128)},...) custom-call(s32[64]{0:T(128)} %partner.1, ...), custom_call_target="tpu_custom_call" | custom-call | tf_op jit(solution)/shard_map/select/pallas_call | solution.py:524

commit v4 on v3

--- a/solution.py
+++ b/solution.py
@@ -37,11 +37,16 @@
     return pl.ds(pl.multiple_of((w * 9 + slot) * UNIT + first, 16), count)
 
 
+def tile(t):
+    return pl.ds(t * TILE, TILE)
+
+
 def kernel(
-    tok, acc, rt, gt, wg, wu, wd, ms, fm, sm,
+    tok_hbm, acc, rt, gt, wg, wu, wd, ms, fm, sm,
     out, ng, nu, nd, nm, nf, nsd,
-    w_g, w_u, w_d, gat, pck, rcv, ret, ring, fin, meta_y, meta_in, meta, pick, wt_hi, wt_lo, hid,
+    tok, tok_sem, w_g, w_u, w_d, gat, pck, rcv, ret, ring, fin, meta_y, meta_in, meta, pick, wt_hi, wt_lo, hid,
     ys, yr, yms, ymr, zs, zr, zms, zmr, xs, xr, bs, br, is_, ir, fs, fr, ls, ws, wr, ms_s, ms_r,
+    yts, ytr, oxs, oxr, obs, obr, rts, rtr,
 ):
     e = lax.axis_index("expert")
     q = lax.axis_index("zero")
@@ -64,6 +69,9 @@
     peers += [at(dz=1), at(dz=-1), at(dc=1)]
     for dev in peers:
         pl.semaphore_signal(barrier, inc=1, device_id=dev, device_id_type=MESH)
+
+    tok_copy = pltpu.make_async_copy(tok_hbm, tok, tok_sem)
+    tok_copy.start()
 
     r128 = lax.broadcasted_iota(jnp.int32, (TOK, TOK), 0)
     c128 = lax.broadcasted_iota(jnp.int32, (TOK, TOK), 1)
@@ -78,9 +86,36 @@
     sel = jnp.where((rank_row == i32r) & (acc_row > 0.5), 1.0, 0.0).astype(BF)
     pick[...] = sel
     own_block = unit_rows(0, OWN, 0, ACC)
+    tok_copy.wait()
     for n in range(NT):
         cols = slice(n * TILE, (n + 1) * TILE)
         gat[own_block, cols] = jnp.dot(sel, tok[:, cols], preferred_element_type=F32).astype(BF)
+    pl.semaphore_wait(barrier, len(peers))
+
+    y_meta, y_rows = [], []
+    for n in (1, 2, 3):
+        dev = at(dy=-STEP[n])
+        dst = unit_rows(n // 2, OWN, (n % 2) * ACC, ACC)
+        y_meta.append(remote(meta_y.at[n], meta_in.at[n - 1], yms.at[n - 1], ymr.at[n - 1], dev))
+        if n > 1:
+            y_rows.append(remote(gat.at[own_block], gat.at[dst], ys.at[n - 2], yr.at[n - 2], dev))
+    first_block = unit_rows(0, OWN, ACC, ACC)
+
+    def y_first(t):
+        src, dst = gat.at[own_block, tile(t)], gat.at[first_block, tile(t)]
+        return remote(src, dst, yts.at[t], ytr.at[t], at(dy=-STEP[1]))
+
+    for t in range(NT):
+        y_first(t).start()
+
+    def z_block(b, to, dz):
+        src, dst = unit_rows(0, OWN, b * ACC, ACC), unit_rows(0, to, b * ACC, ACC)
+        n = to if b == 0 else 8 + to
+        return remote(gat.at[src], gat.at[dst], zs.at[0, n], zr.at[0, n], at(dz=dz))
+
+    z_block(0, 0, 1).start()
+    z_block(0, 1, -1).start()
+
     wide = lax.broadcasted_iota(jnp.int32, (TOK, NY * TOK), 1)
     offset = (wide // TOK) * (TOK + ACC)
     here = (rank_col + offset.astype(F32) == wide.astype(F32)) & (acc_col > 0.5)
@@ -95,21 +130,6 @@
         part = placed[:, j * TOK : (j + 1) * TOK]
         meta_y[j, 0:8, :] = part[0:8]
         meta_y[j, 8:16, :] = part[8:16] + part[16:24] + part[24:32]
-
-    for w in range(2):
-        ring[ring_rows(w, 6), :] = jnp.zeros((UNIT, D), BF)
-        ring[ring_rows(w, 4, ACC, ACC), :] = jnp.zeros((ACC, D), BF)
-        ring[ring_rows(w, 5, 0, ACC), :] = jnp.zeros((ACC, D), BF)
-
-    pl.semaphore_wait(barrier, len(peers))
-
-    y_meta, y_rows = [], []
-    for n in (1, 2, 3):
-        dev = at(dy=-STEP[n])
-        dst = unit_rows(n // 2, OWN, (n % 2) * ACC, ACC)
-        y_meta.append(remote(meta_y.at[n], meta_in.at[n - 1], yms.at[n - 1], ymr.at[n - 1], dev))
-        y_rows.append(remote(gat.at[own_block], gat.at[dst], ys.at[n - 1], yr.at[n - 1], dev))
-    y_rows[0].start()
     for cp in y_meta:
         cp.start()
 
@@ -136,23 +156,11 @@
     def z_meta(p, to, dz):
         return remote(meta.at[p], meta.at[to], zms.at[to], zmr.at[to], at(dz=dz))
 
-    def z_block(b, to, dz):
-        src, dst = unit_rows(0, OWN, b * ACC, ACC), unit_rows(0, to, b * ACC, ACC)
-        n = to if b == 0 else 8 + to
-        return remote(gat.at[src], gat.at[dst], zs.at[0, n], zr.at[0, n], at(dz=dz))
-
-    z_block(0, 0, 1).start()
-    z_block(0, 1, -1).start()
     for cp in y_meta:
         cp.wait_recv()
     meta[OWN] = meta_y[0] + meta_in[0] + meta_in[1] + meta_in[2]
     z_meta(OWN, 0, 1).start()
     z_meta(OWN, 1, -1).start()
-    y_rows[0].wait_recv()
-    z_block(1, 0, 1).start()
-    z_block(1, 1, -1).start()
-    for cp in y_rows[1:]:
-        cp.start()
 
     base = (e - x).astype(F32)
 
@@ -164,7 +172,15 @@
         r = unit_rows(w, p, i * GROUP, GROUP)
         return remote(rcv.at[r], ret.at[r], bs.at[w * 8 + p, i - 1], br.at[w * 8 + p, i - 1], at(dx=-i))
 
-    def pack(w, p):
+    def own_send(i, t):
+        r = unit_rows(0, OWN, i * GROUP, GROUP)
+        return remote(pck.at[r, tile(t)], rcv.at[r, tile(t)], oxs.at[i - 1, t], oxr.at[i - 1, t], at(dx=i))
+
+    def own_back(w, i, t):
+        r = unit_rows(w, OWN, i * GROUP, GROUP)
+        return remote(rcv.at[r, tile(t)], ret.at[r, tile(t)], obs.at[w, i - 1, t], obr.at[w, i - 1, t], at(dx=-i))
+
+    def plan(w, p):
         m = meta[p]
         m = jnp.where(w == 0, m, pltpu.roll(m, UNIT, 1))
         routes, gates = m[0:8], m[8:16]
@@ -191,21 +207,39 @@
         place = jnp.concatenate(ones, axis=0).astype(BF)[:, 0:UNIT]
         wt_hi[w * 8 + p] = jnp.concatenate(his, axis=0).astype(BF)
         wt_lo[w * 8 + p] = jnp.concatenate(los, axis=0).astype(BF)
+        return place
+
+    def pack_tile(w, p, place, cols):
+        v = jnp.dot(place, gat[unit_rows(w, p), cols], preferred_element_type=F32).astype(BF)
+        rcv[unit_rows(w, p, 0, GROUP), cols] = v[:GROUP]
+        pck[unit_rows(w, p, GROUP, UNIT - GROUP), cols] = v[GROUP:]
+
+    def pack(w, p):
+        place = plan(w, p)
 
         @pl.loop(0, NT)
         def _(n):
-            cols = pl.ds(pl.multiple_of(n * TILE, TILE), TILE)
-            v = jnp.dot(place, gat[unit_rows(w, p), cols], preferred_element_type=F32).astype(BF)
-            rcv[unit_rows(w, p, 0, GROUP), cols] = v[:GROUP]
-            pck[unit_rows(w, p, GROUP, UNIT - GROUP), cols] = v[GROUP:]
+            pack_tile(w, p, place, pl.ds(pl.multiple_of(n * TILE, TILE), TILE))
 
         for i in (1, 2, 3):
             x_send(w, p, i).start()
 
     def expert(w, p):
-        for d in range(2):
+        for i in (1, 2, 3):
+            x_send(w, p, i).wait_recv()
+        whole = (w == 1) | (p + 1 != OWN)
+
+        @pl.when(whole)
+        def _():
             for i in (1, 2, 3):
-                x_send(w, p + d, i).wait_recv()
+                x_send(w, p + 1, i).wait_recv()
+
+        @pl.when(jnp.logical_not(whole))
+        def _():
+            for i in (1, 2, 3):
+                for t in range(NT):
+                    own_send(i, t).wait_recv()
+
         rows = rcv[unit_rows(w, p, 0, 2 * UNIT), :]
         gate = jnp.dot(rows, w_g[...], preferred_element_type=F32)
         up = jnp.dot(rows, w_u[...], preferred_element_type=F32)
@@ -223,34 +257,52 @@
         for i in (1, 2, 3):
             x_back(w, p, i).start()
 
+    def add_tile(w, p, slots, cols):
+        hi, lo = wt_hi[w * 8 + p][:, 0:UNIT], wt_lo[w * 8 + p][:, 0:UNIT]
+        part = ret[unit_rows(w, p), cols]
+        dims = (((0,), (0,)), ((), ()))
+        v = lax.dot_general(hi, part, dims, preferred_element_type=F32)
+        v = v + lax.dot_general(lo, part, dims, preferred_element_type=F32)
+        for s in slots:
+            v = v + ring[ring_rows(w, s), cols].astype(F32)
+        ring[ring_rows(w, slots[0]), cols] = v.astype(BF)
+
     def combine(w, p, slots):
         for i in (1, 2, 3):
             x_back(w, p, i).wait_recv()
-        hi, lo = wt_hi[w * 8 + p][:, 0:UNIT], wt_lo[w * 8 + p][:, 0:UNIT]
 
         @pl.loop(0, NT)
         def _(n):
-            cols = pl.ds(pl.multiple_of(n * TILE, TILE), TILE)
-            part = ret[unit_rows(w, p), cols]
-            dims = (((0,), (0,)), ((), ()))
-            v = lax.dot_general(hi, part, dims, preferred_element_type=F32)
-            v = v + lax.dot_general(lo, part, dims, preferred_element_type=F32)
-            for s in slots:
-                v = v + ring[ring_rows(w, s), cols].astype(F32)
-            ring[ring_rows(w, slots[0]), cols] = v.astype(BF)
+            add_tile(w, p, slots, pl.ds(pl.multiple_of(n * TILE, TILE), TILE))
 
     def r_rows(w, p, to, dz):
         return remote(ring.at[ring_rows(w, p)], ring.at[ring_rows(w, to)], is_.at[w, to], ir.at[w, to], at(dz=dz))
+
+    def r_tile(w, p, t, dz):
+        src, dst = ring.at[ring_rows(w, p), tile(t)], ring.at[ring_rows(w, OWN + p), tile(t)]
+        return remote(src, dst, rts.at[w, p, t], rtr.at[w, p, t], at(dz=dz))
 
     def r_half(w, h):
         src, dst = ring_rows(w, 6, h * ACC, ACC), ring_rows(w, 4 + h, h * ACC, ACC)
         return remote(ring.at[src], ring.at[dst], is_.at[w, 4 + h], ir.at[w, 4 + h], at(dz=2 * h - 1))
 
-    def y_sum(n):
-        src = ring_rows(n // 2, OWN, (n % 2) * ACC, ACC)
-        return remote(ring.at[src], fin.at[n - 1], fs.at[n - 1], fr.at[n - 1], at(dy=STEP[n]))
-
-    pack(0, OWN)
+    def y_sum(n, t):
+        src, cols = ring_rows(n // 2, OWN, (n % 2) * ACC, ACC), pl.ds(t * TILE, TILE)
+        return remote(
+            ring.at[src, cols], fin.at[n - 1, :, cols], fs.at[n - 1, t], fr.at[n - 1, t], at(dy=STEP[n])
+        )
+
+    place = plan(0, OWN)
+    for t in range(NT):
+        y_first(t).wait_recv()
+        if t == NT - 1:
+            z_block(1, 0, 1).start()
+            z_block(1, 1, -1).start()
+            for cp in y_rows:
+                cp.start()
+        pack_tile(0, OWN, place, tile(t))
+        for i in (1, 2, 3):
+            own_send(i, t).start()
 
     m_copies = []
     for i, (src, dst) in enumerate(((wg, ng), (wu, nu), (wd, nd), (ms, nm), (fm, nf), (sm, nsd))):
@@ -258,9 +310,14 @@
     for cp in m_copies:
         cp.start()
 
-    for cp in y_rows[1:]:
+    for cp in y_rows:
         cp.wait_recv()
     pack(1, OWN)
+    for w in range(2):
+        ring[ring_rows(w, 6), :] = jnp.zeros((UNIT, D), BF)
+        ring[ring_rows(w, 4, ACC, ACC), :] = jnp.zeros((ACC, D), BF)
+        ring[ring_rows(w, 5, 0, ACC), :] = jnp.zeros((ACC, D), BF)
+
     for cp in w_copies[0::2]:
         cp.wait()
     for cp in w_copies[1::2]:
@@ -327,9 +384,9 @@
             def _(d):
                 pack(w, first + d)
 
-        @pl.when(i >= 9)
-        def _():
-            send_back_step(i - 9)
+        @pl.when((i == 8) | (i == 9))
+        def _():
+            send_back_step(i - 8)
 
         @pl.when(i >= 3)
         def _():
@@ -356,7 +413,9 @@
 
         @pl.when(r >= 8)
         def _():
-            send_back(r - 8, OWN)
+            for t in range(NT):
+                for i in (1, 2, 3):
+                    own_back(r - 8, i, t).start()
 
     def return_step(r, carry):
         w, s = wave_and_distance(r)
@@ -383,26 +442,33 @@
                 def _():
                     r_rows(w, p, p, dz).wait_recv()
 
-                combine(w, p, (p,))
-                r_rows(w, p, jnp.where(p >= 2, p - 2, OWN + p), dz).start()
+                @pl.when(s > 1)
+                def _():
+                    combine(w, p, (p,))
+                    r_rows(w, p, p - 2, dz).start()
+
+                @pl.when(s == 1)
+                def _():
+                    for i in (1, 2, 3):
+                        x_back(w, p, i).wait_recv()
+                    for t in range(NT):
+                        add_tile(w, p, (p,), tile(t))
+                        r_tile(w, p, t, dz).start()
 
         return carry
 
     lax.fori_loop(1, 11, tick, 0)
     lax.fori_loop(0, 8, return_step, 0)
 
-    @pl.loop(0, 2)
-    def _(w):
-        r_rows(w, 0, OWN, -1).wait_recv()
-        r_rows(w, 1, OWN + 1, 1).wait_recv()
-        combine(w, OWN, (OWN, OWN + 1))
-
-        @pl.when(w == 0)
-        def _():
-            y_sum(1).start()
-
-    y_sum(2).start()
-    y_sum(3).start()
+    for w in range(2):
+        for t in range(NT):
+            r_tile(w, 0, t, -1).wait_recv()
+            r_tile(w, 1, t, 1).wait_recv()
+            for i in (1, 2, 3):
+                own_back(w, i, t).wait_recv()
+            add_tile(w, OWN, (OWN, OWN + 1), tile(t))
+            for n in ((1,), (2, 3))[w]:
+                y_sum(n, t).start()
 
     for cp in m_copies:
         cp.wait()
@@ -424,20 +490,32 @@
         for h in range(2):
             z_half(w, h).wait_send()
             r_half(w, h).wait_send()
-        for slot in (0, 1, 2, 3, OWN, OWN + 1):
+        for slot in range(4):
             r_rows(w, 0, slot, 1).wait_send()
-
-        @pl.loop(0, 8)
+        for t in range(NT):
+            for p in range(2):
+                r_tile(w, p, t, 1).wait_send()
+            for i in (1, 2, 3):
+                own_back(w, i, t).wait_send()
+
+        @pl.loop(0, OWN)
         def _(p):
             for i in (1, 2, 3):
                 x_send(w, p, i).wait_send()
                 x_back(w, p, i).wait_send()
 
-    for n in (1, 2, 3):
-        y_sum(n).wait()
+    for i in (1, 2, 3):
+        x_send(1, OWN, i).wait_send()
+        for t in range(NT):
+            own_send(i, t).wait_send()
+    for t in range(NT):
+        y_first(t).wait_send()
+
     dims = (((0,), (0,)), ((), ()))
-    for n in range(NT):
-        cols = slice(n * TILE, (n + 1) * TILE)
+    for t in range(NT):
+        for n in (1, 2, 3):
+            y_sum(n, t).wait()
+        cols = slice(t * TILE, (t + 1) * TILE)
         v = ring[ring_rows(0, OWN, 0, ACC), cols].astype(F32)
         for i in range(3):
             v = v + fin[i, :, cols].astype(F32)
@@ -484,9 +562,11 @@
         kernel,
         out_shape=[jax.ShapeDtypeStruct(tokens.shape, BF)]
         + [jax.ShapeDtypeStruct(a.shape, a.dtype) for a in held],
-        in_specs=[vmem] * 4 + [anywhere] * 6,
+        in_specs=[anywhere] + [vmem] * 3 + [anywhere] * 6,
         out_specs=[vmem] + [anywhere] * 6,
         scratch_shapes=[
+            pltpu.VMEM((TOK, D), BF),
+            dma,
             pltpu.VMEM((D, HID), BF),
             pltpu.VMEM((D, HID), BF),
             pltpu.VMEM((HID, D), BF),
@@ -503,13 +583,17 @@
             pltpu.VMEM((16, UNIT, TOK), BF),
             pltpu.VMEM((16, UNIT, TOK), BF),
             pltpu.VMEM((2 * UNIT, HID), BF),
-            dma((3,)), dma((3,)), dma((3,)), dma((3,)),
+            dma((2,)), dma((2,)), dma((3,)), dma((3,)),
             dma((2, 10)), dma((2, 10)), dma((7,)), dma((7,)),
             dma((16, 3)), dma((16, 3)), dma((16, 3)), dma((16, 3)),
             dma((2, 9)), dma((2, 9)),
-            dma((3,)), dma((3,)),
+            dma((3, NT)), dma((3, NT)),
             dma((3,)), dma((3,)), dma((3,)),
             dma((6,)), dma((6,)),
+            dma((NT,)), dma((NT,)),
+            dma((3, NT)), dma((3, NT)),
+            dma((2, 3, NT)), dma((2, 3, NT)),
+            dma((2, 2, NT)), dma((2, 2, NT)),
         ],
         compiler_params=pltpu.CompilerParams(
             collective_id=0, has_side_effects=True, vmem_limit_bytes=60 << 20

time: 199 us -> 197 us (0.990)
  Pallas kernels: 198 us -> 195 us
    pallas_call x1, Pallas kernels: 191 us -> 189 us  [on_device(): pl.pallas_call(kernel, out_shape=[jax.ShapeDtypeStruct(tokens.shape, BF)]...]
where the time goes in v4:
time: 197 us; the launch traced here: 196 us
  Pallas kernels  195 us (99%)
    pallas_call x1, Pallas kernels, on_device(): pl.pallas_call(kernel, out_shape=[jax.ShapeDtypeStruct(tokens.shape, BF)]...  189 us
    pallas_call x1, Pallas kernels, on_device(): pl.pallas_call(functools.partial(select, count), out_shape=outs, in_specs...  6.39 us

profile of v4, /device:TPU:32, one launch (start us, length us, event | category | flops | bytes accessed | tf_op | source)
XLA Modules:
  0.0 196.1 jit_solution(16226884539887801660)
XLA Ops:
  0.6 189.0 %experts.1 = (bf16[128,3584]{1,0:T(8,128)(2,1)}, bf16[1,3584,256]{2,1,0:T(8,128)(2,1)}, bf16[1,3584,256]{2,1,0:T(8,128)(2,1)}, bf16[1,256,3584]{2,1,0:T(8,128)(2...) custom-call(bf16[128,3584]{1,0:T(8,128)(2,1)} %tok_hbm.1, s32[1,128]{1,0:T(1,128)} %bitcast.5, ...), custom_call_target="tpu_custom_call" | custom-call | flops 22548578304 | bytes 25165824 | tf_op jit(solution)/shard_map/experts/pallas_call | solution.py:561
  189.7 6.4 %select.1 = (bf16[1,3584,256]{2,1,0:T(8,128)(2,1)}, bf16[1,3584,256]{2,1,0:T(8,128)(2,1)}, bf16[1,256,3584]{2,1,0:T(8,128)(2,1)}, f32[1,8,3584]{2,1,0:T(8,128)},...) custom-call(s32[64]{0:T(128)} %partner.1, ...), custom_call_target="tpu_custom_call" | custom-call | tf_op jit(solution)/shard_map/select/pallas_call | solution.py:608

commit v5 on v4

--- a/solution.py
+++ b/solution.py
@@ -307,12 +307,12 @@
     m_copies = []
     for i, (src, dst) in enumerate(((wg, ng), (wu, nu), (wd, nd), (ms, nm), (fm, nf), (sm, nsd))):
         m_copies.append(remote(src, dst, ms_s.at[i], ms_r.at[i], at(dy=2)))
-    for cp in m_copies:
-        cp.start()
 
     for cp in y_rows:
         cp.wait_recv()
     pack(1, OWN)
+    for cp in m_copies:
+        cp.start()
     for w in range(2):
         ring[ring_rows(w, 6), :] = jnp.zeros((UNIT, D), BF)
         ring[ring_rows(w, 4, ACC, ACC), :] = jnp.zeros((ACC, D), BF)

time: 197 us -> 197 us (level)
  no operation moved by 1% of the time
where the time goes in v5:
time: 197 us; the launch traced here: 196 us
  Pallas kernels  195 us (99%)
    pallas_call x1, Pallas kernels, on_device(): pl.pallas_call(kernel, out_shape=[jax.ShapeDtypeStruct(tokens.shape, BF)]...  189 us
    pallas_call x1, Pallas kernels, on_device(): pl.pallas_call(functools.partial(select, count), out_shape=outs, in_specs...  6.38 us

profile of v5, /device:TPU:32, one launch (start us, length us, event | category | flops | bytes accessed | tf_op | source)
XLA Modules:
  0.0 196.0 jit_solution(17003748682562384520)
XLA Ops:
  0.6 189.0 %experts.1 = (bf16[128,3584]{1,0:T(8,128)(2,1)}, bf16[1,3584,256]{2,1,0:T(8,128)(2,1)}, bf16[1,3584,256]{2,1,0:T(8,128)(2,1)}, bf16[1,256,3584]{2,1,0:T(8,128)(2...) custom-call(bf16[128,3584]{1,0:T(8,128)(2,1)} %tok_hbm.1, s32[1,128]{1,0:T(1,128)} %bitcast.5, ...), custom_call_target="tpu_custom_call" | custom-call | flops 22548578304 | bytes 25165824 | tf_op jit(solution)/shard_map/experts/pallas_call | solution.py:561
  189.6 6.4 %select.1 = (bf16[1,3584,256]{2,1,0:T(8,128)(2,1)}, bf16[1,3584,256]{2,1,0:T(8,128)(2,1)}, bf16[1,256,3584]{2,1,0:T(8,128)(2,1)}, f32[1,8,3584]{2,1,0:T(8,128)},...) custom-call(s32[64]{0:T(128)} %partner.1, ...), custom_call_target="tpu_custom_call" | custom-call | tf_op jit(solution)/shard_map/select/pallas_call | solution.py:608
